TPU v7x, 128 devices: a whole 4x4x4 slice. The times are simulated.
128 devices in a mesh: dp: 8 (over x, core), tensor: 16 (over z, y).
Axes of the slice: x: 4, y: 4, z: 4, core: 2. Of those that a mesh axis runs over, the one named last changes fastest.
Arguments:
- grad_attn: bfloat16 [8, 8192, 4096], P('dp', 'tensor'), may hold values from -6 to 6
- error_attn: bfloat16 [8, 8192, 4096], P('dp', 'tensor'), may hold values from -3 to 3
- q_attn: float32 [16, 4096], replicated, may hold values from -0.09375 to 0.09375
Outputs:
- approx_attn: bfloat16 [8192, 4096], P('tensor', 'dp')
- new_error_attn: bfloat16 [8, 8192, 4096], P('dp', 'tensor')
- new_q_attn: float32 [16, 4096], replicated
All inputs are finite; a program needn't handle non-finite values.
Results may differ from a plain program's by a relative error of at most 0.012.
Values sent between devices are 32-bit elements; how exact they have to be, the bound alone decides.
No kernel may reach another device: no remote copies, remote signals or barrier semaphores. Data moves between devices by JAX's collectives and lax.ppermute only.
A program may use at most 64 MiB of HBM per device.

v0:
```python
import jax
import jax.numpy as jnp
from jax import lax
from jax.sharding import PartitionSpec as P


def column_basis(left):

    def column_step(index, basis):
        column = lax.dynamic_slice_in_dim(left, index, 1, 1)
        coeffs = jnp.dot(basis.T, column, precision=lax.Precision.HIGHEST)
        coeffs = lax.psum(coeffs, "tensor")
        remain = column - jnp.dot(basis, coeffs, precision=lax.Precision.HIGHEST)
        norm_sq = lax.psum(jnp.sum(remain * remain), "tensor")
        return lax.dynamic_update_slice_in_dim(basis, remain / jnp.sqrt(norm_sq), index, 1)

    return lax.fori_loop(0, left.shape[1], column_step, jnp.zeros_like(left))


def local(grad_attn, error_attn, q_attn):
    replicas = lax.axis_size("dp")
    merged = (grad_attn[0].astype(jnp.float32) + error_attn[0].astype(jnp.float32)).astype(
        jnp.bfloat16
    )
    factor = q_attn.astype(jnp.bfloat16)
    left = lax.dot_general(
        merged, factor, (((1,), (1,)), ((), ())), preferred_element_type=jnp.float32
    )
    left = lax.psum(left, "dp") / replicas
    basis = column_basis(left)
    basis_b = basis.astype(jnp.bfloat16)
    term = lax.dot_general(
        basis_b, merged, (((0,), (0,)), ((), ())), preferred_element_type=jnp.float32
    )
    right = lax.psum(term, ("dp", "tensor"))
    right = right / replicas
    approx = jnp.dot(basis_b, right.astype(jnp.bfloat16), preferred_element_type=jnp.float32)
    new_error = (merged.astype(jnp.float32) - approx).astype(jnp.bfloat16)
    width = approx.shape[1] // replicas
    own_cols = lax.dynamic_slice_in_dim(approx, lax.axis_index("dp") * width, width, 1)
    return (own_cols.astype(jnp.bfloat16), new_error[None], right)


def solution(mesh):
    placed = (P("dp", "tensor", None), P("dp", "tensor", None), P())
    return jax.shard_map(
        local,
        mesh=mesh,
        in_specs=placed,
        out_specs=(P("tensor", "dp"), P("dp", "tensor", None), P()),
        check_vma=False,
    )
```

profile of v0, /device:TPU:1, one launch (start us, length us, event | category | flops | bytes accessed | tf_op | source)
XLA Modules:
  0.0 1411.9 jit_solution(306783701570011895)
XLA Ops:
  35.5 981.3 %while.13 = (s32[]{:T(128)}, f32[512,16]{0,1:T(8,128)S(1)}, f32[512,16]{0,1:T(8,128)S(1)}, s32[]{:T(128)}, s32[]{:T(128)}) while((s32[]{:T(128)}, f32[512,16]{0,1:T(8,128)S(1)}, f32[512,16]{0,1:T(8,128)S(1)}, s32[]{:T(128)}, s32[]{:T(128)}) %tuple.35), condition=%wide.region_5.0_spmd, body=%wide.region_1.0_spmd.sunk | while | flops 198674 | bytes 80233 | solution.py:17
  35.6 34.8 %psum.40 = f32[16]{0:T(128)S(1)} all-reduce(f32[16]{0:T(128)S(1)} %convolution_bitcast_fusion.3), channel_id=1, replica_groups=mesh['dp'=8,'tensor'=16] {'tensor'}, use_global_device_ids=true, to_apply=%region_2.0 | all-reduce | flops 16 | bytes 128 | tf_op jit(solution)/shard_map/while/body/eval_jaxpr/psum | solution.py:12
  101.6 29.7 %psum.40 = f32[16]{0:T(128)S(1)} all-reduce(f32[16]{0:T(128)S(1)} %convolution_bitcast_fusion.3), channel_id=1, replica_groups=mesh['dp'=8,'tensor'=16] {'tensor'}, use_global_device_ids=true, to_apply=%region_2.0 | all-reduce | flops 16 | bytes 128 | tf_op jit(solution)/shard_map/while/body/eval_jaxpr/psum | solution.py:12
  132.0 29.7 %psum.41 = f32[]{:T(128)} all-reduce(f32[]{:T(128)} %get-tuple-element.98), channel_id=1, replica_groups=mesh['dp'=8,'tensor'=16] {'tensor'}, use_global_device_ids=true, to_apply=%region_4.0 | all-reduce | flops 1 | bytes 8 | tf_op jit(solution)/shard_map/while/body/eval_jaxpr/psum | solution.py:14
  162.6 29.7 %psum.40 = f32[16]{0:T(128)S(1)} all-reduce(f32[16]{0:T(128)S(1)} %convolution_bitcast_fusion.3), channel_id=1, replica_groups=mesh['dp'=8,'tensor'=16] {'tensor'}, use_global_device_ids=true, to_apply=%region_2.0 | all-reduce | flops 16 | bytes 128 | tf_op jit(solution)/shard_map/while/body/eval_jaxpr/psum | solution.py:12
  223.3 30.0 %psum.40 = f32[16]{0:T(128)S(1)} all-reduce(f32[16]{0:T(128)S(1)} %convolution_bitcast_fusion.3), channel_id=1, replica_groups=mesh['dp'=8,'tensor'=16] {'tensor'}, use_global_device_ids=true, to_apply=%region_2.0 | all-reduce | flops 16 | bytes 128 | tf_op jit(solution)/shard_map/while/body/eval_jaxpr/psum | solution.py:12
  284.1 30.0 %psum.40 = f32[16]{0:T(128)S(1)} all-reduce(f32[16]{0:T(128)S(1)} %convolution_bitcast_fusion.3), channel_id=1, replica_groups=mesh['dp'=8,'tensor'=16] {'tensor'}, use_global_device_ids=true, to_apply=%region_2.0 | all-reduce | flops 16 | bytes 128 | tf_op jit(solution)/shard_map/while/body/eval_jaxpr/psum | solution.py:12
  345.2 30.3 %psum.40 = f32[16]{0:T(128)S(1)} all-reduce(f32[16]{0:T(128)S(1)} %convolution_bitcast_fusion.3), channel_id=1, replica_groups=mesh['dp'=8,'tensor'=16] {'tensor'}, use_global_device_ids=true, to_apply=%region_2.0 | all-reduce | flops 16 | bytes 128 | tf_op jit(solution)/shard_map/while/body/eval_jaxpr/psum | solution.py:12
  376.2 29.6 %psum.41 = f32[]{:T(128)} all-reduce(f32[]{:T(128)} %get-tuple-element.98), channel_id=1, replica_groups=mesh['dp'=8,'tensor'=16] {'tensor'}, use_global_device_ids=true, to_apply=%region_4.0 | all-reduce | flops 1 | bytes 8 | tf_op jit(solution)/shard_map/while/body/eval_jaxpr/psum | solution.py:14
  406.7 30.0 %psum.40 = f32[16]{0:T(128)S(1)} all-reduce(f32[16]{0:T(128)S(1)} %convolution_bitcast_fusion.3), channel_id=1, replica_groups=mesh['dp'=8,'tensor'=16] {'tensor'}, use_global_device_ids=true, to_apply=%region_2.0 | all-reduce | flops 16 | bytes 128 | tf_op jit(solution)/shard_map/while/body/eval_jaxpr/psum | solution.py:12
  467.7 29.9 %psum.40 = f32[16]{0:T(128)S(1)} all-reduce(f32[16]{0:T(128)S(1)} %convolution_bitcast_fusion.3), channel_id=1, replica_groups=mesh['dp'=8,'tensor'=16] {'tensor'}, use_global_device_ids=true, to_apply=%region_2.0 | all-reduce | flops 16 | bytes 128 | tf_op jit(solution)/shard_map/while/body/eval_jaxpr/psum | solution.py:12
  528.5 30.2 %psum.40 = f32[16]{0:T(128)S(1)} all-reduce(f32[16]{0:T(128)S(1)} %convolution_bitcast_fusion.3), channel_id=1, replica_groups=mesh['dp'=8,'tensor'=16] {'tensor'}, use_global_device_ids=true, to_apply=%region_2.0 | all-reduce | flops 16 | bytes 128 | tf_op jit(solution)/shard_map/while/body/eval_jaxpr/psum | solution.py:12
  589.4 30.1 %psum.40 = f32[16]{0:T(128)S(1)} all-reduce(f32[16]{0:T(128)S(1)} %convolution_bitcast_fusion.3), channel_id=1, replica_groups=mesh['dp'=8,'tensor'=16] {'tensor'}, use_global_device_ids=true, to_apply=%region_2.0 | all-reduce | flops 16 | bytes 128 | tf_op jit(solution)/shard_map/while/body/eval_jaxpr/psum | solution.py:12
  650.6 29.7 %psum.40 = f32[16]{0:T(128)S(1)} all-reduce(f32[16]{0:T(128)S(1)} %convolution_bitcast_fusion.3), channel_id=1, replica_groups=mesh['dp'=8,'tensor'=16] {'tensor'}, use_global_device_ids=true, to_apply=%region_2.0 | all-reduce | flops 16 | bytes 128 | tf_op jit(solution)/shard_map/while/body/eval_jaxpr/psum | solution.py:12
  711.4 29.7 %psum.40 = f32[16]{0:T(128)S(1)} all-reduce(f32[16]{0:T(128)S(1)} %convolution_bitcast_fusion.3), channel_id=1, replica_groups=mesh['dp'=8,'tensor'=16] {'tensor'}, use_global_device_ids=true, to_apply=%region_2.0 | all-reduce | flops 16 | bytes 128 | tf_op jit(solution)/shard_map/while/body/eval_jaxpr/psum | solution.py:12
  741.9 29.9 %psum.41 = f32[]{:T(128)} all-reduce(f32[]{:T(128)} %get-tuple-element.98), channel_id=1, replica_groups=mesh['dp'=8,'tensor'=16] {'tensor'}, use_global_device_ids=true, to_apply=%region_4.0 | all-reduce | flops 1 | bytes 8 | tf_op jit(solution)/shard_map/while/body/eval_jaxpr/psum | solution.py:14
  772.7 29.5 %psum.40 = f32[16]{0:T(128)S(1)} all-reduce(f32[16]{0:T(128)S(1)} %convolution_bitcast_fusion.3), channel_id=1, replica_groups=mesh['dp'=8,'tensor'=16] {'tensor'}, use_global_device_ids=true, to_apply=%region_2.0 | all-reduce | flops 16 | bytes 128 | tf_op jit(solution)/shard_map/while/body/eval_jaxpr/psum | solution.py:12
  803.0 29.6 %psum.41 = f32[]{:T(128)} all-reduce(f32[]{:T(128)} %get-tuple-element.98), channel_id=1, replica_groups=mesh['dp'=8,'tensor'=16] {'tensor'}, use_global_device_ids=true, to_apply=%region_4.0 | all-reduce | flops 1 | bytes 8 | tf_op jit(solution)/shard_map/while/body/eval_jaxpr/psum | solution.py:14
  833.5 29.8 %psum.40 = f32[16]{0:T(128)S(1)} all-reduce(f32[16]{0:T(128)S(1)} %convolution_bitcast_fusion.3), channel_id=1, replica_groups=mesh['dp'=8,'tensor'=16] {'tensor'}, use_global_device_ids=true, to_apply=%region_2.0 | all-reduce | flops 16 | bytes 128 | tf_op jit(solution)/shard_map/while/body/eval_jaxpr/psum | solution.py:12
  894.3 29.9 %psum.40 = f32[16]{0:T(128)S(1)} all-reduce(f32[16]{0:T(128)S(1)} %convolution_bitcast_fusion.3), channel_id=1, replica_groups=mesh['dp'=8,'tensor'=16] {'tensor'}, use_global_device_ids=true, to_apply=%region_2.0 | all-reduce | flops 16 | bytes 128 | tf_op jit(solution)/shard_map/while/body/eval_jaxpr/psum | solution.py:12
  924.9 29.5 %psum.41 = f32[]{:T(128)} all-reduce(f32[]{:T(128)} %get-tuple-element.98), channel_id=1, replica_groups=mesh['dp'=8,'tensor'=16] {'tensor'}, use_global_device_ids=true, to_apply=%region_4.0 | all-reduce | flops 1 | bytes 8 | tf_op jit(solution)/shard_map/while/body/eval_jaxpr/psum | solution.py:14
  955.3 29.9 %psum.40 = f32[16]{0:T(128)S(1)} all-reduce(f32[16]{0:T(128)S(1)} %convolution_bitcast_fusion.3), channel_id=1, replica_groups=mesh['dp'=8,'tensor'=16] {'tensor'}, use_global_device_ids=true, to_apply=%region_2.0 | all-reduce | flops 16 | bytes 128 | tf_op jit(solution)/shard_map/while/body/eval_jaxpr/psum | solution.py:12
  985.9 30.1 %psum.41 = f32[]{:T(128)} all-reduce(f32[]{:T(128)} %get-tuple-element.98), channel_id=1, replica_groups=mesh['dp'=8,'tensor'=16] {'tensor'}, use_global_device_ids=true, to_apply=%region_4.0 | all-reduce | flops 1 | bytes 8 | tf_op jit(solution)/shard_map/while/body/eval_jaxpr/psum | solution.py:14
  1022.1 366.5 %all-reduce.2.cloned.1.call-done = f32[16,4096]{1,0:T(8,128)} async-done(((f32[16,4096]{1,0:T(8,128)}), f32[16,4096]{1,0:T(8,128)}) %all-reduce.2.cloned.1.call-update) | async-done | bytes 262160 | tf_op jit(solution)/shard_map/psum | solution.py:35
  (89 shorter events, 358.2 us)
Async XLA Ops:
  7.2 1381.4 %all-reduce.2.cloned.1.call-start = ((), (), s32[]{:S(2)}) async-start(), calls=%async_computation | async-start | bytes 524288 | tf_op jit(solution)/shard_map/psum | solution.py:35
  1389.6 4.5 copy-start.1
  1389.6 4.5 copy-start
Sparse Core Ops, SparseCore 0:
  1022.2 366.3 all-reduce.1
where the time goes:
time: 1410 us
  blocking collectives  978 us (69%)
  waiting for transfers between devices  367 us (26%)
  matrix products  28.5 us (2%)
  between operations  14.1 us (1%)
    psum x16, blocking collectives, column_step(): coeffs = lax.psum(coeffs, 'tensor')  483 us
    psum x16, blocking collectives, column_step(): norm_sq = lax.psum(jnp.sum(remain * remain), 'tensor')  471 us
    psum x1, waiting for transfers between devices, local(): right = lax.psum(term, ('dp', 'tensor'))  367 us
  transfers between devices with their start and end apart: 1, of which 1 were waited for; matrix products, arithmetic and copies ran while one was open for 0% of the time, Pallas kernels for 0%

commit v1 on v0

v1 whole, which is shorter than its diff:
```python
import functools

import jax
import jax.numpy as jnp
from jax import lax
from jax.experimental import pallas as pl
from jax.experimental.pallas import tpu as pltpu
from jax.sharding import PartitionSpec as P

F32, BF16 = jnp.float32, jnp.bfloat16
ROWS, COLS, RANK = 512, 4096, 16
LANES = 128
TILES = COLS // LANES
GROUP = 4
GROUPS = RANK // GROUP
LIMIT = 40 * 1024 * 1024


def split3(value):
    high = value.astype(BF16)
    rest = value - high.astype(F32)
    middle = rest.astype(BF16)
    return high, middle, (rest - middle.astype(F32)).astype(BF16)


MERGE_STEPS = 8
MERGE_ROWS = ROWS // MERGE_STEPS


def merge_kernel(grad, error, q, merged, left_t, grad_v, error_v, left_v, sems):
    def copies(i):
        rows = pl.ds(i * MERGE_ROWS, MERGE_ROWS)
        return (
            pltpu.make_async_copy(grad.at[rows], grad_v.at[rows], sems.at[0, i]),
            pltpu.make_async_copy(error.at[rows], error_v.at[rows], sems.at[1, i]),
        )

    for i in range(MERGE_STEPS):
        for copy in copies(i):
            copy.start()
    factor = q[...].astype(BF16)
    for i in range(MERGE_STEPS):
        for copy in copies(i):
            copy.wait()
        rows = pl.ds(i * MERGE_ROWS, MERGE_ROWS)
        block = (grad_v[rows].astype(F32) + error_v[rows].astype(F32)).astype(BF16)
        merged[rows] = block
        left_v[rows] = lax.dot_general(
            block, factor, (((1,), (1,)), ((), ())), preferred_element_type=F32
        )
    left_t[...] = left_v[...].T * 0.125


def merge(grad, error, q):
    return pl.pallas_call(
        merge_kernel,
        out_shape=(
            pltpu.VMEM((ROWS, COLS), BF16),
            pltpu.VMEM((RANK, ROWS), F32),
        ),
        in_specs=[
            pl.BlockSpec(memory_space=pltpu.HBM),
            pl.BlockSpec(memory_space=pltpu.HBM),
            pl.BlockSpec(memory_space=pltpu.VMEM),
        ],
        out_specs=(
            pl.BlockSpec(memory_space=pltpu.VMEM),
            pl.BlockSpec(memory_space=pltpu.VMEM),
        ),
        scratch_shapes=[
            pltpu.VMEM((ROWS, COLS), BF16),
            pltpu.VMEM((ROWS, COLS), BF16),
            pltpu.VMEM((ROWS, RANK), F32),
            pltpu.SemaphoreType.DMA((2, MERGE_STEPS)),
        ],
        compiler_params=pltpu.CompilerParams(vmem_limit_bytes=LIMIT),
        name="merge_left",
    )(grad, error, q)


def right_kernel(own, one, two, three, merged, left_t, parts):
    left = (own[...] + two[...]) + (one[...] + three[...])
    left_t[...] = left
    pieces = jnp.concatenate(split3(left), axis=0)
    for tile in range(0, COLS, 512):
        product = jnp.dot(
            pieces, merged[:, tile : tile + 512], preferred_element_type=F32
        )
        product = (product[2 * RANK :] + product[RANK : 2 * RANK]) + product[:RANK]
        for j in range(4):
            for g in range(GROUPS):
                parts[g * TILES + tile // LANES + j] = product[
                    g * GROUP : (g + 1) * GROUP, j * LANES : (j + 1) * LANES
                ]


def right_product(own, one, two, three, merged):
    return pl.pallas_call(
        right_kernel,
        out_shape=(
            pltpu.VMEM((RANK, ROWS), F32),
            pltpu.VMEM((GROUPS * TILES, GROUP, LANES), F32),
        ),
        in_specs=[pl.BlockSpec(memory_space=pltpu.VMEM)] * 5,
        out_specs=(pl.BlockSpec(memory_space=pltpu.VMEM),) * 2,
        compiler_params=pltpu.CompilerParams(vmem_limit_bytes=LIMIT),
        name="right_parts",
    )(own, one, two, three, merged)


OUT_STEPS = 8
OUT_ROWS = ROWS // OUT_STEPS


def inverse_factor(gram):
    row = lax.broadcasted_iota(jnp.int32, (RANK, RANK), 0)
    col = lax.broadcasted_iota(jnp.int32, (RANK, RANK), 1)
    eye = (row == col).astype(F32)
    work = jnp.concatenate([gram, eye], axis=1)
    rows_at = lax.broadcasted_iota(jnp.int32, (RANK, 1), 0)
    result = jnp.zeros((RANK, 2 * RANK), F32)
    for k in range(RANK):
        pivot_row = work[k : k + 1, :]
        scaled = pivot_row * lax.rsqrt(work[k : k + 1, k : k + 1])
        result = jnp.where(rows_at == k, scaled, result)
        ratio = work[:, k : k + 1] / work[k : k + 1, k : k + 1]
        work = work - jnp.where(rows_at > k, ratio, 0.0) * pivot_row
    return result[:, RANK:]


def finish_kernel(
    place, parts, left_t, q, merged, approx, new_error, right, right_b, error_v, sems
):
    for j in range(TILES):
        for g in range(GROUPS):
            right[g * GROUP : (g + 1) * GROUP, j * LANES : (j + 1) * LANES] = (
                parts[g * TILES + j] * 0.125
            )
    total = right[...]
    factor = q[...].astype(BF16)
    gram = lax.dot_general(
        jnp.concatenate(split3(total), axis=0),
        factor,
        (((1,), (1,)), ((), ())),
        preferred_element_type=F32,
    )
    gram = (gram[2 * RANK :] + gram[RANK : 2 * RANK]) + gram[:RANK]
    inverse = inverse_factor(gram)
    exact = functools.partial(
        jnp.dot, preferred_element_type=F32, precision=lax.Precision.HIGHEST
    )
    total = exact(inverse, total)
    right[...] = total
    right_b[...] = total.astype(BF16)
    basis = exact(inverse, left_t[...]).astype(BF16).T

    def out_copy(i):
        rows = pl.ds(i * OUT_ROWS, OUT_ROWS)
        return pltpu.make_async_copy(error_v.at[rows], new_error.at[rows], sems.at[i])

    columns = pl.ds(pl.multiple_of(place[0] * 512, 512), 512)
    for i in range(OUT_STEPS):
        rows = pl.ds(i * OUT_ROWS, OUT_ROWS)
        block = basis[i * OUT_ROWS : (i + 1) * OUT_ROWS]
        product = jnp.dot(block, right_b[...], preferred_element_type=F32)
        error_v[rows] = (merged[rows].astype(F32) - product).astype(BF16)
        out_copy(i).start()
    approx[...] = jnp.dot(
        basis, right_b[:, columns], preferred_element_type=F32
    ).astype(BF16)
    for i in range(OUT_STEPS):
        out_copy(i).wait()


def finish(place, parts, left_t, q, merged):
    vmem = pl.BlockSpec(memory_space=pltpu.VMEM)
    return pl.pallas_call(
        finish_kernel,
        out_shape=(
            jax.ShapeDtypeStruct((ROWS, 512), BF16),
            jax.ShapeDtypeStruct((ROWS, COLS), BF16),
            jax.ShapeDtypeStruct((RANK, COLS), F32),
        ),
        in_specs=[pl.BlockSpec(memory_space=pltpu.SMEM)] + [vmem] * 4,
        out_specs=(vmem, pl.BlockSpec(memory_space=pltpu.HBM), vmem),
        scratch_shapes=[
            pltpu.VMEM((RANK, COLS), BF16),
            pltpu.VMEM((ROWS, COLS), BF16),
            pltpu.SemaphoreType.DMA((OUT_STEPS,)),
        ],
        compiler_params=pltpu.CompilerParams(vmem_limit_bytes=LIMIT),
        name="finish",
    )(place, parts, left_t, q, merged)


def local(grad_attn, error_attn, q_attn):
    merged, left_t = merge(grad_attn[0], error_attn[0], q_attn)

    def moved(value, pairs):
        return lax.ppermute(value, "dp", pairs)

    pair = left_t + moved(left_t, [(i, i ^ 1) for i in range(8)])
    others = [moved(pair, [(i, (i + 2 * k) % 8) for i in range(8)]) for k in (1, 2, 3)]
    left_t, parts = right_product(pair, *others, merged)
    parts = lax.all_to_all(parts, ("dp", "tensor"), 0, 0, tiled=True)
    chunk = jnp.sum(parts, axis=0, keepdims=True)
    parts = jnp.broadcast_to(chunk, parts.shape)
    parts = lax.all_to_all(parts, ("dp", "tensor"), 0, 0, tiled=True)
    place = lax.axis_index("dp").reshape(1).astype(jnp.int32)
    approx, new_error, right = finish(place, parts, left_t, q_attn, merged)
    return (approx, new_error[None], right)


def solution(mesh):
    placed = (P("dp", "tensor", None), P("dp", "tensor", None), P())
    return jax.shard_map(
        local,
        mesh=mesh,
        in_specs=placed,
        out_specs=(P("tensor", "dp"), P("dp", "tensor", None), P()),
        check_vma=False,
    )
```

time: 1410 us -> 68.5 us (0.05)
  blocking collectives: 978 us -> 21.7 us
  waiting for transfers between devices: 367 us -> 15.9 us
  matrix products: 28.5 us -> 0 us
    psum x33 -> x0, blocking collectives: 978 us -> none  [the longest x16 483 us: column_step(): coeffs = lax.psum(coeffs, 'tensor')]
    psum x1 -> x0, waiting for transfers between devices: 367 us -> none  [local(): right = lax.psum(term, ('dp', 'tensor'))]
    dot_general x35 -> x0, matrix products: 28.5 us -> none  [the longest x16 12 us: column_step(): remain = column - jnp.dot(basis, coeffs, precision=lax.Precision.HIGHEST)]
    all_to_all x0 -> x1, blocking collectives: none -> 21.7 us  [local(): parts = lax.all_to_all(parts, ('dp', 'tensor'), 0, 0, tiled=True)]
  transfers between devices with their start and end apart: 1 -> 5, of which waited for: 1 -> 4; matrix products, arithmetic and copies ran while one was open for 0% -> 0% of each run, Pallas kernels for 0% -> 0%
where the time goes in v1:
time: 68.5 us; the launch traced here: 68.2 us
  blocking collectives  21.7 us (32%)
  waiting for transfers between devices  15.9 us (23%)
  Pallas kernels  10.4 us (15%)
  local copies, waits for them, and re-layouts  10.3 us (15%)
  starting transfers between devices  9.18 us (13%)
    all_to_all x1, blocking collectives, local(): parts = lax.all_to_all(parts, ('dp', 'tensor'), 0, 0, tiled=True)  21.7 us
    all_to_all x1, waiting for transfers between devices, local(): parts = lax.all_to_all(parts, ('dp', 'tensor'), 0, 0, tiled=True)  11.5 us
    unnamed x12, local copies, waits for them, and re-layouts  9.55 us
    pallas_call x1, Pallas kernels, finish(): pl.pallas_call(finish_kernel, out_shape=(jax.ShapeDtypeStruct((ROWS, 512)...  5.67 us
    ppermute x4, starting transfers between devices, moved(): return lax.ppermute(value, 'dp', pairs)  5.19 us
    ppermute x4, waiting for transfers between devices, moved(): return lax.ppermute(value, 'dp', pairs)  4.35 us
    all_to_all x1, starting transfers between devices, local(): parts = lax.all_to_all(parts, ('dp', 'tensor'), 0, 0, tiled=True)  3.99 us
    pallas_call x1, Pallas kernels, merge(): pl.pallas_call(merge_kernel, out_shape=(pltpu.VMEM((ROWS, COLS), BF16), p...  3.93 us
  transfers between devices with their start and end apart: 5, of which 4 were waited for; matrix products, arithmetic and copies ran while one was open for 0% of the time, Pallas kernels for 0%

profile of v1, /device:TPU:1, one launch (start us, length us, event | category | flops | bytes accessed | tf_op | source)
XLA Modules:
  0.0 68.2 jit_solution(10046808241475850063)
XLA Ops:
  0.6 0.0 copy-start.2
  0.6 2.2 %copy-done.2 = bf16[1,512,4096]{2,1,0:T(8,128)(2,1)S(1)} copy-done((bf16[1,512,4096]{2,1,0:T(8,128)(2,1)S(1)}, bf16[1,512,4096]{2,1,0:T(8,128)(2,1)}, u32[]{:S(2)}) %copy-start.2) | copy-done | bytes 4194328
  2.8 2.2 %copy-done.3 = bf16[1,512,4096]{2,1,0:T(8,128)(2,1)S(1)} copy-done((bf16[1,512,4096]{2,1,0:T(8,128)(2,1)S(1)}, bf16[1,512,4096]{2,1,0:T(8,128)(2,1)}, u32[]{:S(2)}) %copy-start.3) | copy-done | bytes 4194328
  5.0 0.9 %copy-done.4 = f32[16,4096]{1,0:T(8,128)S(1)} copy-done((f32[16,4096]{1,0:T(8,128)S(1)}, f32[16,4096]{1,0:T(8,128)}, u32[]{:S(2)}) %copy-start.4) | copy-done | bytes 262168
  6.0 3.9 %merge_left.1 = (bf16[512,4096]{1,0:T(8,128)(2,1)S(1)}, f32[16,512]{1,0:T(8,128)S(1)}) custom-call(bf16[512,4096]{1,0:T(8,128)(2,1)S(1)} %bitcast.4, bf16[512,4096]{1,0:T(8,128)(2,1)S(1)} %bitcast.5, f32[16,4096]{1,0:T(8,128)S(1)} %copy-done.4), custom_call_target="tpu_custom_call" | custom-call | tf_op jit(solution)/shard_map/merge_left/pallas_call | solution.py:55
  9.9 0.0 copy-start.5
  9.9 1.5 %collective-permute-start = (f32[16,512]{1,0:T(8,128)S(1)}, f32[16,512]{1,0:T(8,128)S(1)}, u32[]{:S(2)}, u32[]{:S(2)}) collective-permute-start(f32[16,512]{1,0:T(8,128)S(1)} %get-tuple-element.10), channel_id=1, source_target_pairs={{0,16},{16,0},{32,48},{48,32},{64,80},{80,64},{96,112},{112,96},{1... | collective-permute-start | bytes 98312 | tf_op jit(solution)/shard_map/ppermute | solution.py:200
  11.4 0.9 %collective-permute-done = f32[16,512]{1,0:T(8,128)S(1)} collective-permute-done((f32[16,512]{1,0:T(8,128)S(1)}, f32[16,512]{1,0:T(8,128)S(1)}, u32[]{:S(2)}, u32[]{:S(2)}) %collective-permute-start) | collective-permute-done | bytes 32800 | tf_op jit(solution)/shard_map/ppermute | solution.py:200
  12.3 2.6 %collective-permute-start.3 = (f32[16,512]{1,0:T(8,128)S(1)}, f32[16,512]{1,0:T(8,128)S(1)}, u32[]{:S(2)}, u32[]{:S(2)}) collective-permute-start(f32[16,512]{1,0:T(8,128)S(1)} %add.3.own), channel_id=1, source_target_pairs={{0,96},{16,112},{32,0},{48,16},{64,32},{80,48},{96,64},{112,80},{1... | collective-permute-start | bytes 98312 | tf_op jit(solution)/shard_map/ppermute | solution.py:200
  14.8 0.5 collective-permute-start.2
  15.4 0.6 collective-permute-start.1
  16.0 0.0 collective-permute-done.3.three
  16.0 3.2 %collective-permute-done.2.two = f32[16,512]{1,0:T(8,128)S(1)} collective-permute-done((f32[16,512]{1,0:T(8,128)S(1)}, f32[16,512]{1,0:T(8,128)S(1)}, u32[]{:S(2)}, u32[]{:S(2)}) %collective-permute-start.2) | collective-permute-done | bytes 32800 | tf_op jit(solution)/shard_map/ppermute | solution.py:200
  19.1 0.3 collective-permute-done.1.one
  19.5 0.8 %right_parts.1 = (f32[16,512]{1,0:T(8,128)S(1)}, f32[128,4,128]{2,1,0:T(4,128)S(1)}) custom-call(f32[16,512]{1,0:T(8,128)S(1)} %add.3.own, f32[16,512]{1,0:T(8,128)S(1)} %collective-permute-done.1.one, f32[16,512]{1,0:T(8,128)S(1)} %collective-permute-done.2.two, f32[16,512]{1,0:T(8,128)S(1)} %collective-permute-done.3.three, ...), custom_call_target="tpu_custom_call" | custom-call | tf_op jit(solution)/shard_map/right_parts/pallas_call | solution.py:98
  20.2 2.0 %copy-done = bf16[512,4096]{1,0:T(8,128)(2,1)} copy-done((bf16[512,4096]{1,0:T(8,128)(2,1)}, bf16[512,4096]{1,0:T(8,128)(2,1)S(1)}, u32[]{:S(2)}) %copy-start) | copy-done | bytes 4194328
  22.3 21.7 %all_to_all.10 = f32[128,4,128]{2,1,0:T(4,128)S(1)} all-to-all(f32[128,4,128]{2,1,0:T(4,128)S(1)} %get-tuple-element.12), channel_id=1, replica_groups=mesh['dp'=8,'tensor'=16] {'dp','tensor'}, dimensions={0} | all-to-all | bytes 524288 | tf_op jit(solution)/shard_map/all_to_all | solution.py:205
  43.9 0.1 reduce_sum.9
  44.1 0.7 %broadcast_in_dim.4 = f32[128,4,128]{2,1,0:T(4,128)} broadcast(f32[4,128]{1,0:T(4,128)S(1)} %reduce_sum.9), dimensions={1,2} | broadcast | bytes 264192 | tf_op jit(solution)/shard_map/broadcast_in_dim | solution.py:207
  44.8 4.0 %all-to-all-start.1 = ((f32[128,4,128]{2,1,0:T(4,128)}), f32[128,4,128]{2,1,0:T(4,128)S(1)}, u32[]{:S(2)}, u32[]{:S(2)}) async-start(f32[128,4,128]{2,1,0:T(4,128)} %broadcast_in_dim.4), calls=%async_computation.1 | async-start | bytes 524288 | tf_op jit(solution)/shard_map/all_to_all | solution.py:208
  48.8 11.5 %all-to-all-done.1.parts = f32[128,4,128]{2,1,0:T(4,128)S(1)} async-done(((f32[128,4,128]{2,1,0:T(4,128)}), f32[128,4,128]{2,1,0:T(4,128)S(1)}, u32[]{:S(2)}, u32[]{:S(2)}) %all-to-all-start.1) | async-done | bytes 262176 | tf_op jit(solution)/shard_map/all_to_all | solution.py:208
  60.3 0.0 copy-done.5
  60.3 2.2 %copy-done.1 = bf16[512,4096]{1,0:T(8,128)(2,1)S(1)} copy-done((bf16[512,4096]{1,0:T(8,128)(2,1)S(1)}, bf16[512,4096]{1,0:T(8,128)(2,1)}, u32[]{:S(2)}) %copy-start.1) | copy-done | bytes 4194328
  62.5 5.7 %finish.1 = (bf16[512,512]{1,0:T(8,128)(2,1)}, bf16[512,4096]{1,0:T(8,128)(2,1)}, f32[16,4096]{1,0:T(8,128)}) custom-call(s32[1]{0:T(128)} %bitcast.place, f32[128,4,128]{2,1,0:T(4,128)S(1)} %all-to-all-done.1.parts, f32[16,512]{1,0:T(8,128)S(1)} %get-tuple-element.13.left_t, f32[16,4096]{1,0:T(8,128)S(1)} %copy-done.5, bf16[512,4096]{1,0:T(8,128)(2,1)S(1)} %copy-done.1), custom_call_target="tpu_custom_call" | custom-call | tf_op jit(solution)/shard_map/finish/pallas_call | solution.py:177
  (5 shorter events, 0.0 us)
Async XLA Ops:
  0.6 2.2 %copy-start.2 = (bf16[1,512,4096]{2,1,0:T(8,128)(2,1)S(1)}, bf16[1,512,4096]{2,1,0:T(8,128)(2,1)}, u32[]{:S(2)}) copy-start(bf16[1,512,4096]{2,1,0:T(8,128)(2,1)} %param.3) | copy-start | bytes 12582916
  2.8 2.2 %copy-start.3 = (bf16[1,512,4096]{2,1,0:T(8,128)(2,1)S(1)}, bf16[1,512,4096]{2,1,0:T(8,128)(2,1)}, u32[]{:S(2)}) copy-start(bf16[1,512,4096]{2,1,0:T(8,128)(2,1)} %param.4) | copy-start | bytes 12582916
  5.0 0.9 %copy-start.4 = (f32[16,4096]{1,0:T(8,128)S(1)}, f32[16,4096]{1,0:T(8,128)}, u32[]{:S(2)}) copy-start(f32[16,4096]{1,0:T(8,128)} %q.3) | copy-start | bytes 786436
  9.9 50.4 %copy-start.5 = (f32[16,4096]{1,0:T(8,128)S(1)}, f32[16,4096]{1,0:T(8,128)}, u32[]{:S(2)}) copy-start(f32[16,4096]{1,0:T(8,128)} %q.3) | copy-start | bytes 786436
  9.9 2.4 %collective-permute-start = (f32[16,512]{1,0:T(8,128)S(1)}, f32[16,512]{1,0:T(8,128)S(1)}, u32[]{:S(2)}, u32[]{:S(2)}) collective-permute-start(f32[16,512]{1,0:T(8,128)S(1)} %get-tuple-element.10), channel_id=1, source_target_pairs={{0,16},{16,0},{32,48},{48,32},{64,80},{80,64},{96,112},{112,96},{1... | collective-permute-start | bytes 98312 | tf_op jit(solution)/shard_map/ppermute | solution.py:200
  12.3 3.7 %collective-permute-start.3 = (f32[16,512]{1,0:T(8,128)S(1)}, f32[16,512]{1,0:T(8,128)S(1)}, u32[]{:S(2)}, u32[]{:S(2)}) collective-permute-start(f32[16,512]{1,0:T(8,128)S(1)} %add.3.own), channel_id=1, source_target_pairs={{0,96},{16,112},{32,0},{48,16},{64,32},{80,48},{96,64},{112,80},{1... | collective-permute-start | bytes 98312 | tf_op jit(solution)/shard_map/ppermute | solution.py:200
  14.8 4.3 %collective-permute-start.2 = (f32[16,512]{1,0:T(8,128)S(1)}, f32[16,512]{1,0:T(8,128)S(1)}, u32[]{:S(2)}, u32[]{:S(2)}) collective-permute-start(f32[16,512]{1,0:T(8,128)S(1)} %add.3.own), channel_id=1, source_target_pairs={{0,64},{16,80},{32,96},{48,112},{64,0},{80,16},{96,32},{112,48},{1... | collective-permute-start | bytes 98312 | tf_op jit(solution)/shard_map/ppermute | solution.py:200
  15.4 4.1 %collective-permute-start.1 = (f32[16,512]{1,0:T(8,128)S(1)}, f32[16,512]{1,0:T(8,128)S(1)}, u32[]{:S(2)}, u32[]{:S(2)}) collective-permute-start(f32[16,512]{1,0:T(8,128)S(1)} %add.3.own), channel_id=1, source_target_pairs={{0,32},{16,48},{32,64},{48,80},{64,96},{80,112},{96,0},{112,16},{1... | collective-permute-start | bytes 98312 | tf_op jit(solution)/shard_map/ppermute | solution.py:200
  20.2 2.0 %copy-start = (bf16[512,4096]{1,0:T(8,128)(2,1)}, bf16[512,4096]{1,0:T(8,128)(2,1)S(1)}, u32[]{:S(2)}) copy-start(bf16[512,4096]{1,0:T(8,128)(2,1)S(1)} %get-tuple-element.11.merged) | copy-start | bytes 12582916
  44.8 15.5 %all-to-all-start.1 = ((f32[128,4,128]{2,1,0:T(4,128)}), f32[128,4,128]{2,1,0:T(4,128)S(1)}, u32[]{:S(2)}, u32[]{:S(2)}) async-start(f32[128,4,128]{2,1,0:T(4,128)} %broadcast_in_dim.4), calls=%async_computation.1 | async-start | bytes 524288 | tf_op jit(solution)/shard_map/all_to_all | solution.py:208
  60.3 2.2 %copy-start.1 = (bf16[512,4096]{1,0:T(8,128)(2,1)S(1)}, bf16[512,4096]{1,0:T(8,128)(2,1)}, u32[]{:S(2)}) copy-start(bf16[512,4096]{1,0:T(8,128)(2,1)} %copy-done) | copy-start | bytes 12582916

commit v2 on v1

--- a/solution.py
+++ b/solution.py
@@ -75,7 +75,11 @@
         ],
         compiler_params=pltpu.CompilerParams(vmem_limit_bytes=LIMIT),
         name="merge_left",
-    )(grad, error, q)
+    )(
+        pltpu.with_memory_space_constraint(grad, pltpu.HBM),
+        pltpu.with_memory_space_constraint(error, pltpu.HBM),
+        q,
+    )
 
 
 def right_kernel(own, one, two, three, merged, left_t, parts):
@@ -105,7 +109,23 @@
         out_specs=(pl.BlockSpec(memory_space=pltpu.VMEM),) * 2,
         compiler_params=pltpu.CompilerParams(vmem_limit_bytes=LIMIT),
         name="right_parts",
-    )(own, one, two, three, merged)
+    )(own, one, two, three, pltpu.with_memory_space_constraint(merged, pltpu.VMEM))
+
+
+def sum_kernel(parts, chunks):
+    total = jnp.sum(parts[...], axis=0, keepdims=True)
+    chunks[...] = jnp.broadcast_to(total, chunks.shape)
+
+
+def sum_parts(parts):
+    return pl.pallas_call(
+        sum_kernel,
+        out_shape=pltpu.VMEM(parts.shape, F32),
+        in_specs=[pl.BlockSpec(memory_space=pltpu.VMEM)],
+        out_specs=pl.BlockSpec(memory_space=pltpu.VMEM),
+        compiler_params=pltpu.CompilerParams(vmem_limit_bytes=LIMIT),
+        name="sum_parts",
+    )(pltpu.with_memory_space_constraint(parts, pltpu.VMEM))
 
 
 OUT_STEPS = 8
@@ -129,7 +149,7 @@
 
 
 def finish_kernel(
-    place, parts, left_t, q, merged, approx, new_error, right, right_b, error_v, sems
+    parts, left_t, q, merged, approx, new_error, right, right_b, error_v, sems
 ):
     for j in range(TILES):
         for g in range(GROUPS):
@@ -158,7 +178,7 @@
         rows = pl.ds(i * OUT_ROWS, OUT_ROWS)
         return pltpu.make_async_copy(error_v.at[rows], new_error.at[rows], sems.at[i])
 
-    columns = pl.ds(pl.multiple_of(place[0] * 512, 512), 512)
+    columns = pl.ds(pl.multiple_of(lax.axis_index("dp") * 512, 512), 512)
     for i in range(OUT_STEPS):
         rows = pl.ds(i * OUT_ROWS, OUT_ROWS)
         block = basis[i * OUT_ROWS : (i + 1) * OUT_ROWS]
@@ -172,7 +192,7 @@
         out_copy(i).wait()
 
 
-def finish(place, parts, left_t, q, merged):
+def finish(parts, left_t, q, merged):
     vmem = pl.BlockSpec(memory_space=pltpu.VMEM)
     return pl.pallas_call(
         finish_kernel,
@@ -181,7 +201,7 @@
             jax.ShapeDtypeStruct((ROWS, COLS), BF16),
             jax.ShapeDtypeStruct((RANK, COLS), F32),
         ),
-        in_specs=[pl.BlockSpec(memory_space=pltpu.SMEM)] + [vmem] * 4,
+        in_specs=[vmem] * 4,
         out_specs=(vmem, pl.BlockSpec(memory_space=pltpu.HBM), vmem),
         scratch_shapes=[
             pltpu.VMEM((RANK, COLS), BF16),
@@ -190,7 +210,7 @@
         ],
         compiler_params=pltpu.CompilerParams(vmem_limit_bytes=LIMIT),
         name="finish",
-    )(place, parts, left_t, q, merged)
+    )(parts, left_t, q, pltpu.with_memory_space_constraint(merged, pltpu.VMEM))
 
 
 def local(grad_attn, error_attn, q_attn):
@@ -203,11 +223,9 @@
     others = [moved(pair, [(i, (i + 2 * k) % 8) for i in range(8)]) for k in (1, 2, 3)]
     left_t, parts = right_product(pair, *others, merged)
     parts = lax.all_to_all(parts, ("dp", "tensor"), 0, 0, tiled=True)
-    chunk = jnp.sum(parts, axis=0, keepdims=True)
-    parts = jnp.broadcast_to(chunk, parts.shape)
+    parts = sum_parts(parts)
     parts = lax.all_to_all(parts, ("dp", "tensor"), 0, 0, tiled=True)
-    place = lax.axis_index("dp").reshape(1).astype(jnp.int32)
-    approx, new_error, right = finish(place, parts, left_t, q_attn, merged)
+    approx, new_error, right = finish(parts, left_t, q_attn, merged)
     return (approx, new_error[None], right)
 
 

time: 68.5 us -> 59.4 us (0.87)
  blocking collectives: 21.7 us -> 36.9 us
  waiting for transfers between devices: 15.9 us -> 4.35 us
  local copies, waits for them, and re-layouts: 10.3 us -> 0.95 us
  starting transfers between devices: 9.18 us -> 5.19 us
  Pallas kernels: 10.4 us -> 11.2 us
    all_to_all x1 -> x2, blocking collectives: 21.7 us -> 36.9 us  [local(): parts = lax.all_to_all(parts, ('dp', 'tensor'), 0, 0, tiled=True)]
    all_to_all x1 -> x0, waiting for transfers between devices: 11.5 us -> none  [local(): parts = lax.all_to_all(parts, ('dp', 'tensor'), 0, 0, tiled=True)]
    unnamed x12 -> x4, local copies, waits for them, and re-layouts: 9.55 us -> 0.95 us
    all_to_all x1 -> x0, starting transfers between devices: 3.99 us -> none  [local(): parts = lax.all_to_all(parts, ('dp', 'tensor'), 0, 0, tiled=True)]
    broadcast_in_dim x1 -> x0, local copies, waits for them, and re-layouts: 0.74 us -> none  [local(): parts = jnp.broadcast_to(chunk, parts.shape)]
  transfers between devices with their start and end apart: 5 -> 4, of which waited for: 4 -> 3; matrix products, arithmetic and copies ran while one was open for 0% -> 0% of each run, Pallas kernels for 0% -> 0%
where the time goes in v2:
time: 59.4 us; the launch traced here: 59.2 us
  blocking collectives  36.9 us (62%)
  Pallas kernels  11.2 us (19%)
  starting transfers between devices  5.19 us (9%)
  waiting for transfers between devices  4.35 us (7%)
  local copies, waits for them, and re-layouts  0.95 us (2%)
  between operations  0.66 us (1%)
    all_to_all x2, blocking collectives, local(): parts = lax.all_to_all(parts, ('dp', 'tensor'), 0, 0, tiled=True)  36.9 us
    pallas_call x1, Pallas kernels, finish(): pl.pallas_call(finish_kernel, out_shape=(jax.ShapeDtypeStruct((ROWS, 512)...  5.67 us
    ppermute x4, starting transfers between devices, moved(): return lax.ppermute(value, 'dp', pairs)  5.19 us
    pallas_call x1, Pallas kernels, merge(): pl.pallas_call(merge_kernel, out_shape=(pltpu.VMEM((ROWS, COLS), BF16), p...  4.54 us
    ppermute x4, waiting for transfers between devices, moved(): return lax.ppermute(value, 'dp', pairs)  4.35 us
  transfers between devices with their start and end apart: 4, of which 3 were waited for; matrix products, arithmetic and copies ran while one was open for 0% of the time, Pallas kernels for 0%

profile of v2, /device:TPU:1, one launch (start us, length us, event | category | flops | bytes accessed | tf_op | source)
XLA Modules:
  0.0 59.2 jit_solution(10140105150995708448)
XLA Ops:
  0.6 0.0 copy-start
  0.6 0.9 %copy-done = f32[16,4096]{1,0:T(8,128)S(1)} copy-done((f32[16,4096]{1,0:T(8,128)S(1)}, f32[16,4096]{1,0:T(8,128)}, u32[]{:S(2)}) %copy-start) | copy-done | bytes 262168
  1.6 4.5 %merge_left.1 = (bf16[512,4096]{1,0:T(8,128)(2,1)S(1)}, f32[16,512]{1,0:T(8,128)S(1)}) custom-call(bf16[512,4096]{1,0:T(8,128)(2,1)} %bitcast.3, bf16[512,4096]{1,0:T(8,128)(2,1)} %bitcast.4, f32[16,4096]{1,0:T(8,128)S(1)} %copy-done), custom_call_target="tpu_custom_call" | custom-call | tf_op jit(solution)/shard_map/merge_left/pallas_call | solution.py:55
  6.1 0.0 copy-start.1
  6.1 1.5 %collective-permute-start = (f32[16,512]{1,0:T(8,128)S(1)}, f32[16,512]{1,0:T(8,128)S(1)}, u32[]{:S(2)}, u32[]{:S(2)}) collective-permute-start(f32[16,512]{1,0:T(8,128)S(1)} %get-tuple-element.10), channel_id=1, source_target_pairs={{0,16},{16,0},{32,48},{48,32},{64,80},{80,64},{96,112},{112,96},{1... | collective-permute-start | bytes 98312 | tf_op jit(solution)/shard_map/ppermute | solution.py:220
  7.6 0.9 %collective-permute-done = f32[16,512]{1,0:T(8,128)S(1)} collective-permute-done((f32[16,512]{1,0:T(8,128)S(1)}, f32[16,512]{1,0:T(8,128)S(1)}, u32[]{:S(2)}, u32[]{:S(2)}) %collective-permute-start) | collective-permute-done | bytes 32800 | tf_op jit(solution)/shard_map/ppermute | solution.py:220
  8.5 2.6 %collective-permute-start.3 = (f32[16,512]{1,0:T(8,128)S(1)}, f32[16,512]{1,0:T(8,128)S(1)}, u32[]{:S(2)}, u32[]{:S(2)}) collective-permute-start(f32[16,512]{1,0:T(8,128)S(1)} %add.3.own), channel_id=1, source_target_pairs={{0,96},{16,112},{32,0},{48,16},{64,32},{80,48},{96,64},{112,80},{1... | collective-permute-start | bytes 98312 | tf_op jit(solution)/shard_map/ppermute | solution.py:220
  11.1 0.5 collective-permute-start.2
  11.6 0.6 %collective-permute-start.1 = (f32[16,512]{1,0:T(8,128)S(1)}, f32[16,512]{1,0:T(8,128)S(1)}, u32[]{:S(2)}, u32[]{:S(2)}) collective-permute-start(f32[16,512]{1,0:T(8,128)S(1)} %add.3.own), channel_id=1, source_target_pairs={{0,32},{16,48},{32,64},{48,80},{64,96},{80,112},{96,0},{112,16},{1... | collective-permute-start | bytes 98312 | tf_op jit(solution)/shard_map/ppermute | solution.py:220
  12.2 0.0 collective-permute-done.3.three
  12.2 3.1 %collective-permute-done.2.two = f32[16,512]{1,0:T(8,128)S(1)} collective-permute-done((f32[16,512]{1,0:T(8,128)S(1)}, f32[16,512]{1,0:T(8,128)S(1)}, u32[]{:S(2)}, u32[]{:S(2)}) %collective-permute-start.2) | collective-permute-done | bytes 32800 | tf_op jit(solution)/shard_map/ppermute | solution.py:220
  15.4 0.3 collective-permute-done.1.one
  15.7 0.8 %right_parts.1 = (f32[16,512]{1,0:T(8,128)S(1)}, f32[128,4,128]{2,1,0:T(4,128)S(1)}) custom-call(f32[16,512]{1,0:T(8,128)S(1)} %add.3.own, f32[16,512]{1,0:T(8,128)S(1)} %collective-permute-done.1.one, f32[16,512]{1,0:T(8,128)S(1)} %collective-permute-done.2.two, f32[16,512]{1,0:T(8,128)S(1)} %collective-permute-done.3.three, ...), custom_call_target="tpu_custom_call" | custom-call | tf_op jit(solution)/shard_map/right_parts/pallas_call | solution.py:102
  16.5 21.7 %all_to_all.10.parts = f32[128,4,128]{2,1,0:T(4,128)S(1)} all-to-all(f32[128,4,128]{2,1,0:T(4,128)S(1)} %get-tuple-element.12), channel_id=1, replica_groups=mesh['dp'=8,'tensor'=16] {'dp','tensor'}, dimensions={0} | all-to-all | bytes 524288 | tf_op jit(solution)/shard_map/all_to_all | solution.py:225
  38.1 0.2 sum_parts.1
  38.3 15.2 %all_to_all.11.parts = f32[128,4,128]{2,1,0:T(4,128)S(1)} all-to-all(f32[128,4,128]{2,1,0:T(4,128)S(1)} %sum_parts.1), channel_id=1, replica_groups=mesh['dp'=8,'tensor'=16] {'dp','tensor'}, dimensions={0} | all-to-all | bytes 524288 | tf_op jit(solution)/shard_map/all_to_all | solution.py:227
  53.6 0.0 copy-done.1
  53.6 5.7 %finish.1 = (bf16[512,512]{1,0:T(8,128)(2,1)}, bf16[512,4096]{1,0:T(8,128)(2,1)}, f32[16,4096]{1,0:T(8,128)}) custom-call(f32[128,4,128]{2,1,0:T(4,128)S(1)} %all_to_all.11.parts, f32[16,512]{1,0:T(8,128)S(1)} %get-tuple-element.13.left_t, f32[16,4096]{1,0:T(8,128)S(1)} %copy-done.1, bf16[512,4096]{1,0:T(8,128)(2,1)S(1)} %get-tuple-element.11.merged), custom_call_target="tpu_custom_call" | custom-call | tf_op jit(solution)/shard_map/finish/pallas_call | solution.py:197
  (1 shorter events, 0.0 us)
Async XLA Ops:
  0.6 1.0 %copy-start = (f32[16,4096]{1,0:T(8,128)S(1)}, f32[16,4096]{1,0:T(8,128)}, u32[]{:S(2)}) copy-start(f32[16,4096]{1,0:T(8,128)} %q.3) | copy-start | bytes 786436
  6.1 47.4 %copy-start.1 = (f32[16,4096]{1,0:T(8,128)S(1)}, f32[16,4096]{1,0:T(8,128)}, u32[]{:S(2)}) copy-start(f32[16,4096]{1,0:T(8,128)} %q.3) | copy-start | bytes 786436
  6.1 2.4 %collective-permute-start = (f32[16,512]{1,0:T(8,128)S(1)}, f32[16,512]{1,0:T(8,128)S(1)}, u32[]{:S(2)}, u32[]{:S(2)}) collective-permute-start(f32[16,512]{1,0:T(8,128)S(1)} %get-tuple-element.10), channel_id=1, source_target_pairs={{0,16},{16,0},{32,48},{48,32},{64,80},{80,64},{96,112},{112,96},{1... | collective-permute-start | bytes 98312 | tf_op jit(solution)/shard_map/ppermute | solution.py:220
  8.5 3.7 %collective-permute-start.3 = (f32[16,512]{1,0:T(8,128)S(1)}, f32[16,512]{1,0:T(8,128)S(1)}, u32[]{:S(2)}, u32[]{:S(2)}) collective-permute-start(f32[16,512]{1,0:T(8,128)S(1)} %add.3.own), channel_id=1, source_target_pairs={{0,96},{16,112},{32,0},{48,16},{64,32},{80,48},{96,64},{112,80},{1... | collective-permute-start | bytes 98312 | tf_op jit(solution)/shard_map/ppermute | solution.py:220
  11.1 4.3 %collective-permute-start.2 = (f32[16,512]{1,0:T(8,128)S(1)}, f32[16,512]{1,0:T(8,128)S(1)}, u32[]{:S(2)}, u32[]{:S(2)}) collective-permute-start(f32[16,512]{1,0:T(8,128)S(1)} %add.3.own), channel_id=1, source_target_pairs={{0,64},{16,80},{32,96},{48,112},{64,0},{80,16},{96,32},{112,48},{1... | collective-permute-start | bytes 98312 | tf_op jit(solution)/shard_map/ppermute | solution.py:220
  11.6 4.1 %collective-permute-start.1 = (f32[16,512]{1,0:T(8,128)S(1)}, f32[16,512]{1,0:T(8,128)S(1)}, u32[]{:S(2)}, u32[]{:S(2)}) collective-permute-start(f32[16,512]{1,0:T(8,128)S(1)} %add.3.own), channel_id=1, source_target_pairs={{0,32},{16,48},{32,64},{48,80},{64,96},{80,112},{96,0},{112,16},{1... | collective-permute-start | bytes 98312 | tf_op jit(solution)/shard_map/ppermute | solution.py:220

commit v3 on v2

v3 whole, which is shorter than its diff:
```python
import functools

import jax
import jax.numpy as jnp
from jax import lax
from jax.experimental import pallas as pl
from jax.experimental.pallas import tpu as pltpu
from jax.sharding import PartitionSpec as P

F32, BF16 = jnp.float32, jnp.bfloat16
ROWS, COLS, RANK = 512, 4096, 16
LANES = 128
TILES = COLS // LANES
GROUP = 4
GROUPS = RANK // GROUP
LIMIT = 40 * 1024 * 1024


def split3(value):
    high = value.astype(BF16)
    rest = value - high.astype(F32)
    middle = rest.astype(BF16)
    return high, middle, (rest - middle.astype(F32)).astype(BF16)


BLOCKS = ((0, 1024), (1024, 1024), (2048, 1024), (3072, 512), (3584, 256), (3840, 256))


def merge_kernel(
    grad, error, q, merged, left_t, factor, grad_v, error_v, q_v, sems, q_sem
):
    def copies(i):
        start, width = BLOCKS[i]
        columns = pl.ds(start, width)
        return (
            pltpu.make_async_copy(
                grad.at[:, columns], grad_v.at[:, columns], sems.at[0, i]
            ),
            pltpu.make_async_copy(
                error.at[:, columns], error_v.at[:, columns], sems.at[1, i]
            ),
        )

    q_copy = pltpu.make_async_copy(q, q_v, q_sem)
    q_copy.start()
    for copy in copies(0):
        copy.start()
    q_copy.wait()
    for i in range(1, len(BLOCKS)):
        for copy in copies(i):
            copy.start()
    factor[...] = q_v[...].astype(BF16)
    left = None
    for i, (start, width) in enumerate(BLOCKS):
        for copy in copies(i):
            copy.wait()
        columns = pl.ds(start, width)
        block = (grad_v[:, columns].astype(F32) + error_v[:, columns].astype(F32)).astype(BF16)
        merged[:, columns] = block
        term = lax.dot_general(
            factor[:, columns],
            block,
            (((1,), (1,)), ((), ())),
            preferred_element_type=F32,
        )
        left = term if left is None else left + term
    left_t[...] = left * 0.125


def merge(grad, error, q):
    hbm = pl.BlockSpec(memory_space=pltpu.HBM)
    vmem = pl.BlockSpec(memory_space=pltpu.VMEM)
    return pl.pallas_call(
        merge_kernel,
        out_shape=(
            pltpu.VMEM((ROWS, COLS), BF16),
            pltpu.VMEM((RANK, ROWS), F32),
            pltpu.VMEM((RANK, COLS), BF16),
        ),
        in_specs=[hbm] * 3,
        out_specs=(vmem, vmem, vmem),
        scratch_shapes=[
            pltpu.VMEM((ROWS, COLS), BF16),
            pltpu.VMEM((ROWS, COLS), BF16),
            pltpu.VMEM((RANK, COLS), F32),
            pltpu.SemaphoreType.DMA((2, len(BLOCKS))),
            pltpu.SemaphoreType.DMA,
        ],
        compiler_params=pltpu.CompilerParams(vmem_limit_bytes=LIMIT),
        name="merge_left",
    )(*(pltpu.with_memory_space_constraint(x, pltpu.HBM) for x in (grad, error, q)))


def right_kernel(own, one, two, three, merged, left_t, parts):
    left = (own[...] + one[...]) + (two[...] + three[...])
    left_t[...] = left
    pieces = jnp.concatenate(split3(left), axis=0)
    for tile in range(0, COLS, 512):
        product = jnp.dot(
            pieces, merged[:, tile : tile + 512], preferred_element_type=F32
        )
        product = (product[2 * RANK :] + product[RANK : 2 * RANK]) + product[:RANK]
        for j in range(4):
            for g in range(GROUPS):
                parts[g * TILES + tile // LANES + j] = product[
                    g * GROUP : (g + 1) * GROUP, j * LANES : (j + 1) * LANES
                ]


def right_product(own, one, two, three, merged):
    return pl.pallas_call(
        right_kernel,
        out_shape=(
            pltpu.VMEM((RANK, ROWS), F32),
            pltpu.VMEM((GROUPS * TILES, GROUP, LANES), F32),
        ),
        in_specs=[pl.BlockSpec(memory_space=pltpu.VMEM)] * 5,
        out_specs=(pl.BlockSpec(memory_space=pltpu.VMEM),) * 2,
        compiler_params=pltpu.CompilerParams(vmem_limit_bytes=LIMIT),
        name="right_parts",
    )(own, one, two, three, pltpu.with_memory_space_constraint(merged, pltpu.VMEM))


def sum_kernel(parts, chunks):
    total = jnp.sum(parts[...], axis=0, keepdims=True)
    chunks[...] = jnp.broadcast_to(total, chunks.shape)


def sum_parts(parts):
    return pl.pallas_call(
        sum_kernel,
        out_shape=pltpu.VMEM(parts.shape, F32),
        in_specs=[pl.BlockSpec(memory_space=pltpu.VMEM)],
        out_specs=pl.BlockSpec(memory_space=pltpu.VMEM),
        compiler_params=pltpu.CompilerParams(vmem_limit_bytes=LIMIT),
        name="sum_parts",
    )(pltpu.with_memory_space_constraint(parts, pltpu.VMEM))


OWN = COLS // 8
OUT_STEPS = COLS // OWN


def inverse_factor(gram):
    row = lax.broadcasted_iota(jnp.int32, (RANK, RANK), 0)
    col = lax.broadcasted_iota(jnp.int32, (RANK, RANK), 1)
    eye = (row == col).astype(F32)
    work = jnp.concatenate([gram, eye], axis=1)
    rows_at = lax.broadcasted_iota(jnp.int32, (RANK, 1), 0)
    result = jnp.zeros((RANK, 2 * RANK), F32)
    for k in range(RANK):
        pivot_row = work[k : k + 1, :]
        scaled = pivot_row * lax.rsqrt(work[k : k + 1, k : k + 1])
        result = jnp.where(rows_at == k, scaled, result)
        ratio = work[:, k : k + 1] / work[k : k + 1, k : k + 1]
        work = work - jnp.where(rows_at > k, ratio, 0.0) * pivot_row
    return result[:, RANK:]


def stacked(left, right):
    a, b, c = split3(left)
    x, y, z = split3(right)
    return (
        jnp.concatenate([c, b, a, b, a, a], axis=1),
        jnp.concatenate([x, y, z, x, y, x], axis=0),
    )


def finish_kernel(
    parts, left_t, factor, merged, approx, new_error, right,
    total_v, right_v, approx_v, error_v, sems, approx_sem, right_sem,
):
    for j in range(TILES):
        for g in range(GROUPS):
            total_v[g * GROUP : (g + 1) * GROUP, j * LANES : (j + 1) * LANES] = (
                parts[g * TILES + j] * 0.125
            )
    gram = lax.dot_general(
        jnp.concatenate(split3(total_v[...]), axis=0),
        factor[...],
        (((1,), (1,)), ((), ())),
        preferred_element_type=F32,
    )
    gram = (gram[2 * RANK :] + gram[RANK : 2 * RANK]) + gram[:RANK]
    inverse = inverse_factor(gram)
    lhs, rhs = stacked(inverse, left_t[...])
    basis = jnp.dot(lhs, rhs, preferred_element_type=F32).astype(BF16).T
    place = lax.axis_index("dp")

    def error_copy(step):
        columns = pl.ds(pl.multiple_of(lax.rem(place + step, OUT_STEPS) * OWN, OWN), OWN)
        return pltpu.make_async_copy(
            error_v.at[:, columns], new_error.at[:, columns], sems.at[step]
        )

    approx_copy = pltpu.make_async_copy(approx_v, approx, approx_sem)
    right_copy = pltpu.make_async_copy(right_v, right, right_sem)
    for step in range(OUT_STEPS):
        columns = pl.ds(pl.multiple_of(lax.rem(place + step, OUT_STEPS) * OWN, OWN), OWN)
        lhs, rhs = stacked(inverse, total_v[:, columns])
        block = jnp.dot(lhs, rhs, preferred_element_type=F32)
        right_v[:, columns] = block
        product = jnp.dot(basis, block.astype(BF16), preferred_element_type=F32)
        error_v[:, columns] = (merged[:, columns].astype(F32) - product).astype(BF16)
        error_copy(step).start()
        if step == 0:
            approx_v[...] = product.astype(BF16)
            approx_copy.start()
    right_copy.start()
    for step in range(OUT_STEPS):
        error_copy(step).wait()
    approx_copy.wait()
    right_copy.wait()


def finish(parts, left_t, factor, merged):
    vmem = pl.BlockSpec(memory_space=pltpu.VMEM)
    hbm = pl.BlockSpec(memory_space=pltpu.HBM)
    return pl.pallas_call(
        finish_kernel,
        out_shape=(
            jax.ShapeDtypeStruct((ROWS, OWN), BF16),
            jax.ShapeDtypeStruct((ROWS, COLS), BF16),
            jax.ShapeDtypeStruct((RANK, COLS), F32),
        ),
        in_specs=[vmem] * 4,
        out_specs=(hbm, hbm, hbm),
        scratch_shapes=[
            pltpu.VMEM((RANK, COLS), F32),
            pltpu.VMEM((RANK, COLS), F32),
            pltpu.VMEM((ROWS, OWN), BF16),
            pltpu.VMEM((ROWS, COLS), BF16),
            pltpu.SemaphoreType.DMA((OUT_STEPS,)),
            pltpu.SemaphoreType.DMA,
            pltpu.SemaphoreType.DMA,
        ],
        compiler_params=pltpu.CompilerParams(vmem_limit_bytes=LIMIT),
        name="finish",
    )(parts, left_t, factor, pltpu.with_memory_space_constraint(merged, pltpu.VMEM))


def local(grad_attn, error_attn, q_attn):
    merged, left_t, factor = merge(grad_attn[0], error_attn[0], q_attn)

    def moved(value, pairs):
        return lax.ppermute(value, "dp", pairs)

    pair = left_t + moved(left_t, [(i, i ^ 1) for i in range(8)])
    others = [moved(pair, [(i, i ^ (2 * k)) for i in range(8)]) for k in (1, 2, 3)]
    left_t, parts = right_product(pair, *others, merged)
    parts = lax.all_to_all(parts, ("dp", "tensor"), 0, 0, tiled=True)
    parts = sum_parts(parts)
    parts = lax.all_to_all(parts, ("dp", "tensor"), 0, 0, tiled=True)
    approx, new_error, right = finish(parts, left_t, factor, merged)
    return (approx, new_error[None], right)


def solution(mesh):
    placed = (P("dp", "tensor", None), P("dp", "tensor", None), P())
    return jax.shard_map(
        local,
        mesh=mesh,
        in_specs=placed,
        out_specs=(P("tensor", "dp"), P("dp", "tensor", None), P()),
        check_vma=False,
    )
```

time: 59.4 us -> 57.7 us (0.971)
  local copies, waits for them, and re-layouts: 0.95 us -> 0 us
  Pallas kernels: 11.2 us -> 10.4 us
    unnamed x4 -> x0, local copies, waits for them, and re-layouts: 0.95 us -> none
    pallas_call x1, Pallas kernels: 5.67 us -> 4.85 us  [finish(): pl.pallas_call(finish_kernel, out_shape=(jax.ShapeDtypeStruct((ROWS, OWN)...]
where the time goes in v3:
time: 57.7 us; the launch traced here: 57.5 us
  blocking collectives  37.3 us (65%)
  Pallas kernels  10.4 us (18%)
  starting transfers between devices  4.75 us (8%)
  waiting for transfers between devices  4.44 us (8%)
  between operations  0.65 us (1%)
    all_to_all x2, blocking collectives, local(): parts = lax.all_to_all(parts, ('dp', 'tensor'), 0, 0, tiled=True)  37.3 us
    pallas_call x1, Pallas kernels, finish(): pl.pallas_call(finish_kernel, out_shape=(jax.ShapeDtypeStruct((ROWS, OWN)...  4.85 us
    ppermute x4, starting transfers between devices, moved(): return lax.ppermute(value, 'dp', pairs)  4.75 us
    pallas_call x1, Pallas kernels, merge(): pl.pallas_call(merge_kernel, out_shape=(pltpu.VMEM((ROWS, COLS), BF16), p...  4.57 us
    ppermute x4, waiting for transfers between devices, moved(): return lax.ppermute(value, 'dp', pairs)  4.44 us
  transfers between devices with their start and end apart: 4, of which 3 were waited for; matrix products, arithmetic and copies ran while one was open for 0% of the time, Pallas kernels for 0%

profile of v3, /device:TPU:1, one launch (start us, length us, event | category | flops | bytes accessed | tf_op | source)
XLA Modules:
  0.0 57.5 jit_solution(6588897176365756556)
XLA Ops:
  0.6 4.6 %merge_left.1 = (bf16[512,4096]{1,0:T(8,128)(2,1)S(1)}, f32[16,512]{1,0:T(8,128)S(1)}, bf16[16,4096]{1,0:T(8,128)(2,1)S(1)}) custom-call(bf16[512,4096]{1,0:T(8,128)(2,1)} %bitcast.3, bf16[512,4096]{1,0:T(8,128)(2,1)} %bitcast.4, f32[16,4096]{1,0:T(8,128)} %q.1), custom_call_target="tpu_custom_call" | custom-call | tf_op jit(solution)/shard_map/merge_left/pallas_call | solution.py:73
  5.2 1.5 %collective-permute-start = (f32[16,512]{1,0:T(8,128)S(1)}, f32[16,512]{1,0:T(8,128)S(1)}, u32[]{:S(2)}, u32[]{:S(2)}) collective-permute-start(f32[16,512]{1,0:T(8,128)S(1)} %get-tuple-element.11), channel_id=1, source_target_pairs={{0,16},{16,0},{32,48},{48,32},{64,80},{80,64},{96,112},{112,96},{1... | collective-permute-start | bytes 98312 | tf_op jit(solution)/shard_map/ppermute | solution.py:246
  6.7 0.9 %collective-permute-done = f32[16,512]{1,0:T(8,128)S(1)} collective-permute-done((f32[16,512]{1,0:T(8,128)S(1)}, f32[16,512]{1,0:T(8,128)S(1)}, u32[]{:S(2)}, u32[]{:S(2)}) %collective-permute-start) | collective-permute-done | bytes 32800 | tf_op jit(solution)/shard_map/ppermute | solution.py:246
  7.6 2.6 %collective-permute-start.3 = (f32[16,512]{1,0:T(8,128)S(1)}, f32[16,512]{1,0:T(8,128)S(1)}, u32[]{:S(2)}, u32[]{:S(2)}) collective-permute-start(f32[16,512]{1,0:T(8,128)S(1)} %add.3.own), channel_id=1, source_target_pairs={{0,96},{16,112},{32,64},{48,80},{64,32},{80,48},{96,0},{112,16},{1... | collective-permute-start | bytes 98312 | tf_op jit(solution)/shard_map/ppermute | solution.py:246
  10.1 0.5 collective-permute-start.2
  10.7 0.2 collective-permute-start.1
  10.8 0.7 %collective-permute-done.3.three = f32[16,512]{1,0:T(8,128)S(1)} collective-permute-done((f32[16,512]{1,0:T(8,128)S(1)}, f32[16,512]{1,0:T(8,128)S(1)}, u32[]{:S(2)}, u32[]{:S(2)}) %collective-permute-start.3) | collective-permute-done | bytes 32800 | tf_op jit(solution)/shard_map/ppermute | solution.py:246
  11.5 2.9 %collective-permute-done.2.two = f32[16,512]{1,0:T(8,128)S(1)} collective-permute-done((f32[16,512]{1,0:T(8,128)S(1)}, f32[16,512]{1,0:T(8,128)S(1)}, u32[]{:S(2)}, u32[]{:S(2)}) %collective-permute-start.2) | collective-permute-done | bytes 32800 | tf_op jit(solution)/shard_map/ppermute | solution.py:246
  14.4 0.0 collective-permute-done.1.one
  14.4 0.8 %right_parts.1 = (f32[16,512]{1,0:T(8,128)S(1)}, f32[128,4,128]{2,1,0:T(4,128)S(1)}) custom-call(f32[16,512]{1,0:T(8,128)S(1)} %add.3.own, f32[16,512]{1,0:T(8,128)S(1)} %collective-permute-done.1.one, f32[16,512]{1,0:T(8,128)S(1)} %collective-permute-done.2.two, f32[16,512]{1,0:T(8,128)S(1)} %collective-permute-done.3.three, ...), custom_call_target="tpu_custom_call" | custom-call | tf_op jit(solution)/shard_map/right_parts/pallas_call | solution.py:111
  15.2 22.0 %all_to_all.10.parts = f32[128,4,128]{2,1,0:T(4,128)S(1)} all-to-all(f32[128,4,128]{2,1,0:T(4,128)S(1)} %get-tuple-element.13), channel_id=1, replica_groups=mesh['dp'=8,'tensor'=16] {'dp','tensor'}, dimensions={0} | all-to-all | bytes 524288 | tf_op jit(solution)/shard_map/all_to_all | solution.py:251
  37.2 0.2 sum_parts.1
  37.4 15.2 %all_to_all.11.parts = f32[128,4,128]{2,1,0:T(4,128)S(1)} all-to-all(f32[128,4,128]{2,1,0:T(4,128)S(1)} %sum_parts.1), channel_id=1, replica_groups=mesh['dp'=8,'tensor'=16] {'dp','tensor'}, dimensions={0} | all-to-all | bytes 524288 | tf_op jit(solution)/shard_map/all_to_all | solution.py:253
  52.6 4.9 %finish.1 = (bf16[512,512]{1,0:T(8,128)(2,1)}, bf16[512,4096]{1,0:T(8,128)(2,1)}, f32[16,4096]{1,0:T(8,128)}) custom-call(f32[128,4,128]{2,1,0:T(4,128)S(1)} %all_to_all.11.parts, f32[16,512]{1,0:T(8,128)S(1)} %get-tuple-element.14.left_t, bf16[16,4096]{1,0:T(8,128)(2,1)S(1)} %get-tuple-element.15.factor, bf16[512,4096]{1,0:T(8,128)(2,1)S(1)} %get-tuple-element.12.merged), custom_call_target="tpu_custom_call" | custom-call | tf_op jit(solution)/shard_map/finish/pallas_call | solution.py:219
  (1 shorter events, 0.0 us)
Async XLA Ops:
  5.2 2.4 %collective-permute-start = (f32[16,512]{1,0:T(8,128)S(1)}, f32[16,512]{1,0:T(8,128)S(1)}, u32[]{:S(2)}, u32[]{:S(2)}) collective-permute-start(f32[16,512]{1,0:T(8,128)S(1)} %get-tuple-element.11), channel_id=1, source_target_pairs={{0,16},{16,0},{32,48},{48,32},{64,80},{80,64},{96,112},{112,96},{1... | collective-permute-start | bytes 98312 | tf_op jit(solution)/shard_map/ppermute | solution.py:246
  7.6 4.0 %collective-permute-start.3 = (f32[16,512]{1,0:T(8,128)S(1)}, f32[16,512]{1,0:T(8,128)S(1)}, u32[]{:S(2)}, u32[]{:S(2)}) collective-permute-start(f32[16,512]{1,0:T(8,128)S(1)} %add.3.own), channel_id=1, source_target_pairs={{0,96},{16,112},{32,64},{48,80},{64,32},{80,48},{96,0},{112,16},{1... | collective-permute-start | bytes 98312 | tf_op jit(solution)/shard_map/ppermute | solution.py:246
  10.1 4.3 %collective-permute-start.2 = (f32[16,512]{1,0:T(8,128)S(1)}, f32[16,512]{1,0:T(8,128)S(1)}, u32[]{:S(2)}, u32[]{:S(2)}) collective-permute-start(f32[16,512]{1,0:T(8,128)S(1)} %add.3.own), channel_id=1, source_target_pairs={{0,64},{16,80},{32,96},{48,112},{64,0},{80,16},{96,32},{112,48},{1... | collective-permute-start | bytes 98312 | tf_op jit(solution)/shard_map/ppermute | solution.py:246
  10.7 3.8 %collective-permute-start.1 = (f32[16,512]{1,0:T(8,128)S(1)}, f32[16,512]{1,0:T(8,128)S(1)}, u32[]{:S(2)}, u32[]{:S(2)}) collective-permute-start(f32[16,512]{1,0:T(8,128)S(1)} %add.3.own), channel_id=1, source_target_pairs={{0,32},{16,48},{32,0},{48,16},{64,96},{80,112},{96,64},{112,80},{1... | collective-permute-start | bytes 98312 | tf_op jit(solution)/shard_map/ppermute | solution.py:246

commit v4 on v3

--- a/solution.py
+++ b/solution.py
@@ -142,18 +142,21 @@
 
 
 def inverse_factor(gram):
+    width = 2 * RANK
     row = lax.broadcasted_iota(jnp.int32, (RANK, RANK), 0)
     col = lax.broadcasted_iota(jnp.int32, (RANK, RANK), 1)
-    eye = (row == col).astype(F32)
-    work = jnp.concatenate([gram, eye], axis=1)
-    rows_at = lax.broadcasted_iota(jnp.int32, (RANK, 1), 0)
-    result = jnp.zeros((RANK, 2 * RANK), F32)
+    work = jnp.concatenate([gram, (row == col).astype(F32)], axis=1)
+    rows_at = lax.broadcasted_iota(jnp.int32, (RANK, width), 0)
+    columns = [jnp.broadcast_to(gram[:, k : k + 1], (RANK, width)) for k in range(RANK)]
+    result = jnp.zeros((RANK, width), F32)
     for k in range(RANK):
-        pivot_row = work[k : k + 1, :]
-        scaled = pivot_row * lax.rsqrt(work[k : k + 1, k : k + 1])
-        result = jnp.where(rows_at == k, scaled, result)
-        ratio = work[:, k : k + 1] / work[k : k + 1, k : k + 1]
-        work = work - jnp.where(rows_at > k, ratio, 0.0) * pivot_row
+        pivot = jnp.broadcast_to(columns[k][k : k + 1], (RANK, width))
+        pivot_row = jnp.broadcast_to(work[k : k + 1], (RANK, width))
+        result = jnp.where(rows_at == k, pivot_row * lax.rsqrt(pivot), result)
+        ratio = jnp.where(rows_at > k, columns[k], 0.0) / pivot
+        work = work - ratio * pivot_row
+        for j in range(k + 1, RANK):
+            columns[j] = columns[j] - ratio * columns[j][k : k + 1]
     return result[:, RANK:]
 
 

time: 57.7 us -> 56.6 us (0.981)
  Pallas kernels: 10.4 us -> 9.35 us
    pallas_call x1, Pallas kernels: 4.85 us -> 3.84 us  [finish(): pl.pallas_call(finish_kernel, out_shape=(jax.ShapeDtypeStruct((ROWS, OWN)...]
where the time goes in v4:
time: 56.6 us; the launch traced here: 56.5 us
  blocking collectives  37.3 us (66%)
  Pallas kernels  9.35 us (17%)
  starting transfers between devices  4.75 us (8%)
  waiting for transfers between devices  4.44 us (8%)
  between operations  0.65 us (1%)
    all_to_all x2, blocking collectives, local(): parts = lax.all_to_all(parts, ('dp', 'tensor'), 0, 0, tiled=True)  37.3 us
    ppermute x4, starting transfers between devices, moved(): return lax.ppermute(value, 'dp', pairs)  4.75 us
    pallas_call x1, Pallas kernels, merge(): pl.pallas_call(merge_kernel, out_shape=(pltpu.VMEM((ROWS, COLS), BF16), p...  4.57 us
    ppermute x4, waiting for transfers between devices, moved(): return lax.ppermute(value, 'dp', pairs)  4.44 us
    pallas_call x1, Pallas kernels, finish(): pl.pallas_call(finish_kernel, out_shape=(jax.ShapeDtypeStruct((ROWS, OWN)...  3.84 us
  transfers between devices with their start and end apart: 4, of which 3 were waited for; matrix products, arithmetic and copies ran while one was open for 0% of the time, Pallas kernels for 0%

profile of v4, /device:TPU:1, one launch (start us, length us, event | category | flops | bytes accessed | tf_op | source)
XLA Modules:
  0.0 56.5 jit_solution(5348276286309898419)
XLA Ops:
  0.6 4.6 %merge_left.1 = (bf16[512,4096]{1,0:T(8,128)(2,1)S(1)}, f32[16,512]{1,0:T(8,128)S(1)}, bf16[16,4096]{1,0:T(8,128)(2,1)S(1)}) custom-call(bf16[512,4096]{1,0:T(8,128)(2,1)} %bitcast.3, bf16[512,4096]{1,0:T(8,128)(2,1)} %bitcast.4, f32[16,4096]{1,0:T(8,128)} %q.1), custom_call_target="tpu_custom_call" | custom-call | tf_op jit(solution)/shard_map/merge_left/pallas_call | solution.py:73
  5.2 1.5 %collective-permute-start = (f32[16,512]{1,0:T(8,128)S(1)}, f32[16,512]{1,0:T(8,128)S(1)}, u32[]{:S(2)}, u32[]{:S(2)}) collective-permute-start(f32[16,512]{1,0:T(8,128)S(1)} %get-tuple-element.11), channel_id=1, source_target_pairs={{0,16},{16,0},{32,48},{48,32},{64,80},{80,64},{96,112},{112,96},{1... | collective-permute-start | bytes 98312 | tf_op jit(solution)/shard_map/ppermute | solution.py:249
  6.7 0.9 %collective-permute-done = f32[16,512]{1,0:T(8,128)S(1)} collective-permute-done((f32[16,512]{1,0:T(8,128)S(1)}, f32[16,512]{1,0:T(8,128)S(1)}, u32[]{:S(2)}, u32[]{:S(2)}) %collective-permute-start) | collective-permute-done | bytes 32800 | tf_op jit(solution)/shard_map/ppermute | solution.py:249
  7.6 2.6 %collective-permute-start.3 = (f32[16,512]{1,0:T(8,128)S(1)}, f32[16,512]{1,0:T(8,128)S(1)}, u32[]{:S(2)}, u32[]{:S(2)}) collective-permute-start(f32[16,512]{1,0:T(8,128)S(1)} %add.3.own), channel_id=1, source_target_pairs={{0,96},{16,112},{32,64},{48,80},{64,32},{80,48},{96,0},{112,16},{1... | collective-permute-start | bytes 98312 | tf_op jit(solution)/shard_map/ppermute | solution.py:249
  10.1 0.5 collective-permute-start.2
  10.7 0.2 collective-permute-start.1
  10.8 0.7 %collective-permute-done.3.three = f32[16,512]{1,0:T(8,128)S(1)} collective-permute-done((f32[16,512]{1,0:T(8,128)S(1)}, f32[16,512]{1,0:T(8,128)S(1)}, u32[]{:S(2)}, u32[]{:S(2)}) %collective-permute-start.3) | collective-permute-done | bytes 32800 | tf_op jit(solution)/shard_map/ppermute | solution.py:249
  11.5 2.9 %collective-permute-done.2.two = f32[16,512]{1,0:T(8,128)S(1)} collective-permute-done((f32[16,512]{1,0:T(8,128)S(1)}, f32[16,512]{1,0:T(8,128)S(1)}, u32[]{:S(2)}, u32[]{:S(2)}) %collective-permute-start.2) | collective-permute-done | bytes 32800 | tf_op jit(solution)/shard_map/ppermute | solution.py:249
  14.4 0.0 collective-permute-done.1.one
  14.4 0.8 %right_parts.1 = (f32[16,512]{1,0:T(8,128)S(1)}, f32[128,4,128]{2,1,0:T(4,128)S(1)}) custom-call(f32[16,512]{1,0:T(8,128)S(1)} %add.3.own, f32[16,512]{1,0:T(8,128)S(1)} %collective-permute-done.1.one, f32[16,512]{1,0:T(8,128)S(1)} %collective-permute-done.2.two, f32[16,512]{1,0:T(8,128)S(1)} %collective-permute-done.3.three, ...), custom_call_target="tpu_custom_call" | custom-call | tf_op jit(solution)/shard_map/right_parts/pallas_call | solution.py:111
  15.2 22.0 %all_to_all.10.parts = f32[128,4,128]{2,1,0:T(4,128)S(1)} all-to-all(f32[128,4,128]{2,1,0:T(4,128)S(1)} %get-tuple-element.13), channel_id=1, replica_groups=mesh['dp'=8,'tensor'=16] {'dp','tensor'}, dimensions={0} | all-to-all | bytes 524288 | tf_op jit(solution)/shard_map/all_to_all | solution.py:254
  37.2 0.2 sum_parts.1
  37.4 15.2 %all_to_all.11.parts = f32[128,4,128]{2,1,0:T(4,128)S(1)} all-to-all(f32[128,4,128]{2,1,0:T(4,128)S(1)} %sum_parts.1), channel_id=1, replica_groups=mesh['dp'=8,'tensor'=16] {'dp','tensor'}, dimensions={0} | all-to-all | bytes 524288 | tf_op jit(solution)/shard_map/all_to_all | solution.py:256
  52.6 3.8 %finish.1 = (bf16[512,512]{1,0:T(8,128)(2,1)}, bf16[512,4096]{1,0:T(8,128)(2,1)}, f32[16,4096]{1,0:T(8,128)}) custom-call(f32[128,4,128]{2,1,0:T(4,128)S(1)} %all_to_all.11.parts, f32[16,512]{1,0:T(8,128)S(1)} %get-tuple-element.14.left_t, bf16[16,4096]{1,0:T(8,128)(2,1)S(1)} %get-tuple-element.15.factor, bf16[512,4096]{1,0:T(8,128)(2,1)S(1)} %get-tuple-element.12.merged), custom_call_target="tpu_custom_call" | custom-call | tf_op jit(solution)/shard_map/finish/pallas_call | solution.py:222
  (1 shorter events, 0.0 us)
Async XLA Ops:
  5.2 2.4 %collective-permute-start = (f32[16,512]{1,0:T(8,128)S(1)}, f32[16,512]{1,0:T(8,128)S(1)}, u32[]{:S(2)}, u32[]{:S(2)}) collective-permute-start(f32[16,512]{1,0:T(8,128)S(1)} %get-tuple-element.11), channel_id=1, source_target_pairs={{0,16},{16,0},{32,48},{48,32},{64,80},{80,64},{96,112},{112,96},{1... | collective-permute-start | bytes 98312 | tf_op jit(solution)/shard_map/ppermute | solution.py:249
  7.6 4.0 %collective-permute-start.3 = (f32[16,512]{1,0:T(8,128)S(1)}, f32[16,512]{1,0:T(8,128)S(1)}, u32[]{:S(2)}, u32[]{:S(2)}) collective-permute-start(f32[16,512]{1,0:T(8,128)S(1)} %add.3.own), channel_id=1, source_target_pairs={{0,96},{16,112},{32,64},{48,80},{64,32},{80,48},{96,0},{112,16},{1... | collective-permute-start | bytes 98312 | tf_op jit(solution)/shard_map/ppermute | solution.py:249
  10.1 4.3 %collective-permute-start.2 = (f32[16,512]{1,0:T(8,128)S(1)}, f32[16,512]{1,0:T(8,128)S(1)}, u32[]{:S(2)}, u32[]{:S(2)}) collective-permute-start(f32[16,512]{1,0:T(8,128)S(1)} %add.3.own), channel_id=1, source_target_pairs={{0,64},{16,80},{32,96},{48,112},{64,0},{80,16},{96,32},{112,48},{1... | collective-permute-start | bytes 98312 | tf_op jit(solution)/shard_map/ppermute | solution.py:249
  10.7 3.8 %collective-permute-start.1 = (f32[16,512]{1,0:T(8,128)S(1)}, f32[16,512]{1,0:T(8,128)S(1)}, u32[]{:S(2)}, u32[]{:S(2)}) collective-permute-start(f32[16,512]{1,0:T(8,128)S(1)} %add.3.own), channel_id=1, source_target_pairs={{0,32},{16,48},{32,0},{48,16},{64,96},{80,112},{96,64},{112,80},{1... | collective-permute-start | bytes 98312 | tf_op jit(solution)/shard_map/ppermute | solution.py:249

commit v5 on v4

--- a/solution.py
+++ b/solution.py
@@ -23,7 +23,8 @@
     return high, middle, (rest - middle.astype(F32)).astype(BF16)
 
 
-BLOCKS = ((0, 1024), (1024, 1024), (2048, 1024), (3072, 512), (3584, 256), (3840, 256))
+BLOCKS = ((0, 512), (512, 1024), (1536, 1024), (2560, 1024), (3584, 384), (3968, 128))
+AHEAD = 3
 
 
 def merge_kernel(
@@ -43,17 +44,19 @@
 
     q_copy = pltpu.make_async_copy(q, q_v, q_sem)
     q_copy.start()
-    for copy in copies(0):
-        copy.start()
-    q_copy.wait()
-    for i in range(1, len(BLOCKS)):
+    for i in range(AHEAD):
         for copy in copies(i):
             copy.start()
-    factor[...] = q_v[...].astype(BF16)
     left = None
     for i, (start, width) in enumerate(BLOCKS):
         for copy in copies(i):
             copy.wait()
+        if i + AHEAD < len(BLOCKS):
+            for copy in copies(i + AHEAD):
+                copy.start()
+        if i == 0:
+            q_copy.wait()
+            factor[...] = q_v[...].astype(BF16)
         columns = pl.ds(start, width)
         block = (grad_v[:, columns].astype(F32) + error_v[:, columns].astype(F32)).astype(BF16)
         merged[:, columns] = block
@@ -91,7 +94,23 @@
     )(*(pltpu.with_memory_space_constraint(x, pltpu.HBM) for x in (grad, error, q)))
 
 
-def right_kernel(own, one, two, three, merged, left_t, parts):
+def turn_kernel(factor, factor_t):
+    factor_t[...] = factor[...].T
+
+
+def turned(factor):
+    return pl.pallas_call(
+        turn_kernel,
+        out_shape=pltpu.VMEM((COLS, RANK), BF16),
+        in_specs=[pl.BlockSpec(memory_space=pltpu.VMEM)],
+        out_specs=pl.BlockSpec(memory_space=pltpu.VMEM),
+        compiler_params=pltpu.CompilerParams(vmem_limit_bytes=LIMIT),
+        cost_estimate=pl.CostEstimate(flops=0, bytes_accessed=1 << 20, transcendentals=0),
+        name="turn_factor",
+    )(factor)
+
+
+def right_kernel(own, one, two, three, merged, after, left_t, parts):
     left = (own[...] + one[...]) + (two[...] + three[...])
     left_t[...] = left
     pieces = jnp.concatenate(split3(left), axis=0)
@@ -107,18 +126,19 @@
                 ]
 
 
-def right_product(own, one, two, three, merged):
+def right_product(own, one, two, three, merged, after):
     return pl.pallas_call(
         right_kernel,
         out_shape=(
             pltpu.VMEM((RANK, ROWS), F32),
             pltpu.VMEM((GROUPS * TILES, GROUP, LANES), F32),
         ),
-        in_specs=[pl.BlockSpec(memory_space=pltpu.VMEM)] * 5,
+        in_specs=[pl.BlockSpec(memory_space=pltpu.VMEM)] * 5
+        + [pl.BlockSpec(memory_space=pl.ANY)],
         out_specs=(pl.BlockSpec(memory_space=pltpu.VMEM),) * 2,
         compiler_params=pltpu.CompilerParams(vmem_limit_bytes=LIMIT),
         name="right_parts",
-    )(own, one, two, three, pltpu.with_memory_space_constraint(merged, pltpu.VMEM))
+    )(own, one, two, three, pltpu.with_memory_space_constraint(merged, pltpu.VMEM), after)
 
 
 def sum_kernel(parts, chunks):
@@ -170,8 +190,8 @@
 
 
 def finish_kernel(
-    parts, left_t, factor, merged, approx, new_error, right,
-    total_v, right_v, approx_v, error_v, sems, approx_sem, right_sem,
+    parts, left_t, factor_t, merged, approx, new_error, right,
+    total_v, right_v, right_b, approx_v, error_v, sems, approx_sem, right_sem,
 ):
     for j in range(TILES):
         for g in range(GROUPS):
@@ -180,8 +200,8 @@
             )
     gram = lax.dot_general(
         jnp.concatenate(split3(total_v[...]), axis=0),
-        factor[...],
-        (((1,), (1,)), ((), ())),
+        factor_t[...],
+        (((1,), (0,)), ((), ())),
         preferred_element_type=F32,
     )
     gram = (gram[2 * RANK :] + gram[RANK : 2 * RANK]) + gram[:RANK]
@@ -198,25 +218,26 @@
 
     approx_copy = pltpu.make_async_copy(approx_v, approx, approx_sem)
     right_copy = pltpu.make_async_copy(right_v, right, right_sem)
+    lhs, rhs = stacked(inverse, total_v[...])
+    total = jnp.dot(lhs, rhs, preferred_element_type=F32)
+    right_v[...] = total
+    right_copy.start()
+    right_b[...] = total.astype(BF16)
     for step in range(OUT_STEPS):
         columns = pl.ds(pl.multiple_of(lax.rem(place + step, OUT_STEPS) * OWN, OWN), OWN)
-        lhs, rhs = stacked(inverse, total_v[:, columns])
-        block = jnp.dot(lhs, rhs, preferred_element_type=F32)
-        right_v[:, columns] = block
-        product = jnp.dot(basis, block.astype(BF16), preferred_element_type=F32)
+        product = jnp.dot(basis, right_b[:, columns], preferred_element_type=F32)
         error_v[:, columns] = (merged[:, columns].astype(F32) - product).astype(BF16)
         error_copy(step).start()
         if step == 0:
             approx_v[...] = product.astype(BF16)
             approx_copy.start()
-    right_copy.start()
     for step in range(OUT_STEPS):
         error_copy(step).wait()
     approx_copy.wait()
     right_copy.wait()
 
 
-def finish(parts, left_t, factor, merged):
+def finish(parts, left_t, factor_t, merged):
     vmem = pl.BlockSpec(memory_space=pltpu.VMEM)
     hbm = pl.BlockSpec(memory_space=pltpu.HBM)
     return pl.pallas_call(
@@ -231,6 +252,7 @@
         scratch_shapes=[
             pltpu.VMEM((RANK, COLS), F32),
             pltpu.VMEM((RANK, COLS), F32),
+            pltpu.VMEM((RANK, COLS), BF16),
             pltpu.VMEM((ROWS, OWN), BF16),
             pltpu.VMEM((ROWS, COLS), BF16),
             pltpu.SemaphoreType.DMA((OUT_STEPS,)),
@@ -239,22 +261,23 @@
         ],
         compiler_params=pltpu.CompilerParams(vmem_limit_bytes=LIMIT),
         name="finish",
-    )(parts, left_t, factor, pltpu.with_memory_space_constraint(merged, pltpu.VMEM))
+    )(parts, left_t, factor_t, pltpu.with_memory_space_constraint(merged, pltpu.VMEM))
 
 
 def local(grad_attn, error_attn, q_attn):
     merged, left_t, factor = merge(grad_attn[0], error_attn[0], q_attn)
+    factor_t = turned(factor)
 
     def moved(value, pairs):
         return lax.ppermute(value, "dp", pairs)
 
     pair = left_t + moved(left_t, [(i, i ^ 1) for i in range(8)])
     others = [moved(pair, [(i, i ^ (2 * k)) for i in range(8)]) for k in (1, 2, 3)]
-    left_t, parts = right_product(pair, *others, merged)
+    left_t, parts = right_product(pair, *others, merged, factor_t)
     parts = lax.all_to_all(parts, ("dp", "tensor"), 0, 0, tiled=True)
     parts = sum_parts(parts)
     parts = lax.all_to_all(parts, ("dp", "tensor"), 0, 0, tiled=True)
-    approx, new_error, right = finish(parts, left_t, factor, merged)
+    approx, new_error, right = finish(parts, left_t, factor_t, merged)
     return (approx, new_error[None], right)
 
 

time: 56.6 us -> 56.3 us (level)
  transfers between devices with their start and end apart: 4 -> 4, of which waited for: 3 -> 3; matrix products, arithmetic and copies ran while one was open for 0% -> 0% of each run, Pallas kernels for 0% -> 1%
where the time goes in v5:
time: 56.3 us; the launch traced here: 56.1 us
  blocking collectives  37.3 us (66%)
  Pallas kernels  9.33 us (17%)
  starting transfers between devices  4.75 us (8%)
  waiting for transfers between devices  4.09 us (7%)
  between operations  0.66 us (1%)
    all_to_all x2, blocking collectives, local(): parts = lax.all_to_all(parts, ('dp', 'tensor'), 0, 0, tiled=True)  37.3 us
    ppermute x4, starting transfers between devices, moved(): return lax.ppermute(value, 'dp', pairs)  4.75 us
    pallas_call x1, Pallas kernels, merge(): pl.pallas_call(merge_kernel, out_shape=(pltpu.VMEM((ROWS, COLS), BF16), p...  4.47 us
    ppermute x4, waiting for transfers between devices, moved(): return lax.ppermute(value, 'dp', pairs)  4.09 us
    pallas_call x1, Pallas kernels, finish(): pl.pallas_call(finish_kernel, out_shape=(jax.ShapeDtypeStruct((ROWS, OWN)...  3.58 us
  transfers between devices with their start and end apart: 4, of which 3 were waited for; matrix products, arithmetic and copies ran while one was open for 0% of the time, Pallas kernels for 1%

profile of v5, /device:TPU:1, one launch (start us, length us, event | category | flops | bytes accessed | tf_op | source)
XLA Modules:
  0.0 56.1 jit_solution(8693833429458765965)
XLA Ops:
  0.6 4.5 %merge_left.1 = (bf16[512,4096]{1,0:T(8,128)(2,1)S(1)}, f32[16,512]{1,0:T(8,128)S(1)}, bf16[16,4096]{1,0:T(8,128)(2,1)S(1)}) custom-call(bf16[512,4096]{1,0:T(8,128)(2,1)} %bitcast.3, bf16[512,4096]{1,0:T(8,128)(2,1)} %bitcast.4, f32[16,4096]{1,0:T(8,128)} %q.1), custom_call_target="tpu_custom_call" | custom-call | tf_op jit(solution)/shard_map/merge_left/pallas_call | solution.py:76
  5.1 1.5 %collective-permute-start = (f32[16,512]{1,0:T(8,128)S(1)}, f32[16,512]{1,0:T(8,128)S(1)}, u32[]{:S(2)}, u32[]{:S(2)}) collective-permute-start(f32[16,512]{1,0:T(8,128)S(1)} %get-tuple-element.11), channel_id=1, source_target_pairs={{0,16},{16,0},{32,48},{48,32},{64,80},{80,64},{96,112},{112,96},{1... | collective-permute-start | bytes 98312 | tf_op jit(solution)/shard_map/ppermute | solution.py:272
  6.6 0.9 %collective-permute-done = f32[16,512]{1,0:T(8,128)S(1)} collective-permute-done((f32[16,512]{1,0:T(8,128)S(1)}, f32[16,512]{1,0:T(8,128)S(1)}, u32[]{:S(2)}, u32[]{:S(2)}) %collective-permute-start) | collective-permute-done | bytes 32800 | tf_op jit(solution)/shard_map/ppermute | solution.py:272
  7.5 2.6 %collective-permute-start.3 = (f32[16,512]{1,0:T(8,128)S(1)}, f32[16,512]{1,0:T(8,128)S(1)}, u32[]{:S(2)}, u32[]{:S(2)}) collective-permute-start(f32[16,512]{1,0:T(8,128)S(1)} %add.3.own), channel_id=1, source_target_pairs={{0,96},{16,112},{32,64},{48,80},{64,32},{80,48},{96,0},{112,16},{1... | collective-permute-start | bytes 98312 | tf_op jit(solution)/shard_map/ppermute | solution.py:272
  10.0 0.5 collective-permute-start.2
  10.6 0.2 collective-permute-start.1
  10.7 0.3 turn_factor.1.after.factor_t
  11.1 0.4 collective-permute-done.3.three
  11.5 2.9 %collective-permute-done.2.two = f32[16,512]{1,0:T(8,128)S(1)} collective-permute-done((f32[16,512]{1,0:T(8,128)S(1)}, f32[16,512]{1,0:T(8,128)S(1)}, u32[]{:S(2)}, u32[]{:S(2)}) %collective-permute-start.2) | collective-permute-done | bytes 32800 | tf_op jit(solution)/shard_map/ppermute | solution.py:272
  14.3 0.0 collective-permute-done.1.one
  14.3 0.8 %right_parts.1 = (f32[16,512]{1,0:T(8,128)S(1)}, f32[128,4,128]{2,1,0:T(4,128)S(1)}) custom-call(f32[16,512]{1,0:T(8,128)S(1)} %add.3.own, f32[16,512]{1,0:T(8,128)S(1)} %collective-permute-done.1.one, f32[16,512]{1,0:T(8,128)S(1)} %collective-permute-done.2.two, f32[16,512]{1,0:T(8,128)S(1)} %collective-permute-done.3.three, ...), custom_call_target="tpu_custom_call" | custom-call | tf_op jit(solution)/shard_map/right_parts/pallas_call | solution.py:130
  15.1 22.0 %all_to_all.10.parts = f32[128,4,128]{2,1,0:T(4,128)S(1)} all-to-all(f32[128,4,128]{2,1,0:T(4,128)S(1)} %get-tuple-element.14), channel_id=1, replica_groups=mesh['dp'=8,'tensor'=16] {'dp','tensor'}, dimensions={0} | all-to-all | bytes 524288 | tf_op jit(solution)/shard_map/all_to_all | solution.py:277
  37.1 0.2 sum_parts.1
  37.3 15.2 %all_to_all.11.parts = f32[128,4,128]{2,1,0:T(4,128)S(1)} all-to-all(f32[128,4,128]{2,1,0:T(4,128)S(1)} %sum_parts.1), channel_id=1, replica_groups=mesh['dp'=8,'tensor'=16] {'dp','tensor'}, dimensions={0} | all-to-all | bytes 524288 | tf_op jit(solution)/shard_map/all_to_all | solution.py:279
  52.5 3.6 %finish.1 = (bf16[512,512]{1,0:T(8,128)(2,1)}, bf16[512,4096]{1,0:T(8,128)(2,1)}, f32[16,4096]{1,0:T(8,128)}) custom-call(f32[128,4,128]{2,1,0:T(4,128)S(1)} %all_to_all.11.parts, f32[16,512]{1,0:T(8,128)S(1)} %get-tuple-element.15.left_t, bf16[4096,16]{1,0:T(8,128)(2,1)S(1)} %turn_factor.1.after.factor_t, bf16[512,4096]{1,0:T(8,128)(2,1)S(1)} %get-tuple-element.12.merged), custom_call_target="tpu_custom_call" | custom-call | tf_op jit(solution)/shard_map/finish/pallas_call | solution.py:243
  (1 shorter events, 0.0 us)
Async XLA Ops:
  5.1 2.4 %collective-permute-start = (f32[16,512]{1,0:T(8,128)S(1)}, f32[16,512]{1,0:T(8,128)S(1)}, u32[]{:S(2)}, u32[]{:S(2)}) collective-permute-start(f32[16,512]{1,0:T(8,128)S(1)} %get-tuple-element.11), channel_id=1, source_target_pairs={{0,16},{16,0},{32,48},{48,32},{64,80},{80,64},{96,112},{112,96},{1... | collective-permute-start | bytes 98312 | tf_op jit(solution)/shard_map/ppermute | solution.py:272
  7.5 4.0 %collective-permute-start.3 = (f32[16,512]{1,0:T(8,128)S(1)}, f32[16,512]{1,0:T(8,128)S(1)}, u32[]{:S(2)}, u32[]{:S(2)}) collective-permute-start(f32[16,512]{1,0:T(8,128)S(1)} %add.3.own), channel_id=1, source_target_pairs={{0,96},{16,112},{32,64},{48,80},{64,32},{80,48},{96,0},{112,16},{1... | collective-permute-start | bytes 98312 | tf_op jit(solution)/shard_map/ppermute | solution.py:272
  10.0 4.3 %collective-permute-start.2 = (f32[16,512]{1,0:T(8,128)S(1)}, f32[16,512]{1,0:T(8,128)S(1)}, u32[]{:S(2)}, u32[]{:S(2)}) collective-permute-start(f32[16,512]{1,0:T(8,128)S(1)} %add.3.own), channel_id=1, source_target_pairs={{0,64},{16,80},{32,96},{48,112},{64,0},{80,16},{96,32},{112,48},{1... | collective-permute-start | bytes 98312 | tf_op jit(solution)/shard_map/ppermute | solution.py:272
  10.6 3.8 %collective-permute-start.1 = (f32[16,512]{1,0:T(8,128)S(1)}, f32[16,512]{1,0:T(8,128)S(1)}, u32[]{:S(2)}, u32[]{:S(2)}) collective-permute-start(f32[16,512]{1,0:T(8,128)S(1)} %add.3.own), channel_id=1, source_target_pairs={{0,32},{16,48},{32,0},{48,16},{64,96},{80,112},{96,64},{112,80},{1... | collective-permute-start | bytes 98312 | tf_op jit(solution)/shard_map/ppermute | solution.py:272

commit v6 on v5

--- a/solution.py
+++ b/solution.py
@@ -23,7 +23,7 @@
     return high, middle, (rest - middle.astype(F32)).astype(BF16)
 
 
-BLOCKS = ((0, 512), (512, 1024), (1536, 1024), (2560, 1024), (3584, 384), (3968, 128))
+BLOCKS = ((0, 512), (512, 768), (1280, 1024), (2304, 1024), (3328, 512), (3840, 256))
 AHEAD = 3
 
 

time: 56.3 us -> 56.1 us (level)
  no operation moved by 1% of the time
where the time goes in v6:
time: 56.1 us; the launch traced here: 56 us
  blocking collectives  37.3 us (66%)
  Pallas kernels  9.19 us (16%)
  starting transfers between devices  4.75 us (8%)
  waiting for transfers between devices  4.09 us (7%)
  between operations  0.66 us (1%)
    all_to_all x2, blocking collectives, local(): parts = lax.all_to_all(parts, ('dp', 'tensor'), 0, 0, tiled=True)  37.3 us
    ppermute x4, starting transfers between devices, moved(): return lax.ppermute(value, 'dp', pairs)  4.75 us
    pallas_call x1, Pallas kernels, merge(): pl.pallas_call(merge_kernel, out_shape=(pltpu.VMEM((ROWS, COLS), BF16), p...  4.34 us
    ppermute x4, waiting for transfers between devices, moved(): return lax.ppermute(value, 'dp', pairs)  4.09 us
    pallas_call x1, Pallas kernels, finish(): pl.pallas_call(finish_kernel, out_shape=(jax.ShapeDtypeStruct((ROWS, OWN)...  3.58 us
  transfers between devices with their start and end apart: 4, of which 3 were waited for; matrix products, arithmetic and copies ran while one was open for 0% of the time, Pallas kernels for 1%

profile of v6, /device:TPU:1, one launch (start us, length us, event | category | flops | bytes accessed | tf_op | source)
XLA Modules:
  0.0 56.0 jit_solution(6641777032220421659)
XLA Ops:
  0.6 4.3 %merge_left.1 = (bf16[512,4096]{1,0:T(8,128)(2,1)S(1)}, f32[16,512]{1,0:T(8,128)S(1)}, bf16[16,4096]{1,0:T(8,128)(2,1)S(1)}) custom-call(bf16[512,4096]{1,0:T(8,128)(2,1)} %bitcast.3, bf16[512,4096]{1,0:T(8,128)(2,1)} %bitcast.4, f32[16,4096]{1,0:T(8,128)} %q.1), custom_call_target="tpu_custom_call" | custom-call | tf_op jit(solution)/shard_map/merge_left/pallas_call | solution.py:76
  5.0 1.5 %collective-permute-start = (f32[16,512]{1,0:T(8,128)S(1)}, f32[16,512]{1,0:T(8,128)S(1)}, u32[]{:S(2)}, u32[]{:S(2)}) collective-permute-start(f32[16,512]{1,0:T(8,128)S(1)} %get-tuple-element.11), channel_id=1, source_target_pairs={{0,16},{16,0},{32,48},{48,32},{64,80},{80,64},{96,112},{112,96},{1... | collective-permute-start | bytes 98312 | tf_op jit(solution)/shard_map/ppermute | solution.py:272
  6.5 0.9 %collective-permute-done = f32[16,512]{1,0:T(8,128)S(1)} collective-permute-done((f32[16,512]{1,0:T(8,128)S(1)}, f32[16,512]{1,0:T(8,128)S(1)}, u32[]{:S(2)}, u32[]{:S(2)}) %collective-permute-start) | collective-permute-done | bytes 32800 | tf_op jit(solution)/shard_map/ppermute | solution.py:272
  7.3 2.6 %collective-permute-start.3 = (f32[16,512]{1,0:T(8,128)S(1)}, f32[16,512]{1,0:T(8,128)S(1)}, u32[]{:S(2)}, u32[]{:S(2)}) collective-permute-start(f32[16,512]{1,0:T(8,128)S(1)} %add.3.own), channel_id=1, source_target_pairs={{0,96},{16,112},{32,64},{48,80},{64,32},{80,48},{96,0},{112,16},{1... | collective-permute-start | bytes 98312 | tf_op jit(solution)/shard_map/ppermute | solution.py:272
  9.9 0.5 collective-permute-start.2
  10.4 0.2 collective-permute-start.1
  10.6 0.3 turn_factor.1.after.factor_t
  10.9 0.4 collective-permute-done.3.three
  11.3 2.9 %collective-permute-done.2.two = f32[16,512]{1,0:T(8,128)S(1)} collective-permute-done((f32[16,512]{1,0:T(8,128)S(1)}, f32[16,512]{1,0:T(8,128)S(1)}, u32[]{:S(2)}, u32[]{:S(2)}) %collective-permute-start.2) | collective-permute-done | bytes 32800 | tf_op jit(solution)/shard_map/ppermute | solution.py:272
  14.2 0.0 collective-permute-done.1.one
  14.2 0.8 %right_parts.1 = (f32[16,512]{1,0:T(8,128)S(1)}, f32[128,4,128]{2,1,0:T(4,128)S(1)}) custom-call(f32[16,512]{1,0:T(8,128)S(1)} %add.3.own, f32[16,512]{1,0:T(8,128)S(1)} %collective-permute-done.1.one, f32[16,512]{1,0:T(8,128)S(1)} %collective-permute-done.2.two, f32[16,512]{1,0:T(8,128)S(1)} %collective-permute-done.3.three, ...), custom_call_target="tpu_custom_call" | custom-call | tf_op jit(solution)/shard_map/right_parts/pallas_call | solution.py:130
  14.9 22.0 %all_to_all.10.parts = f32[128,4,128]{2,1,0:T(4,128)S(1)} all-to-all(f32[128,4,128]{2,1,0:T(4,128)S(1)} %get-tuple-element.14), channel_id=1, replica_groups=mesh['dp'=8,'tensor'=16] {'dp','tensor'}, dimensions={0} | all-to-all | bytes 524288 | tf_op jit(solution)/shard_map/all_to_all | solution.py:277
  37.0 0.2 sum_parts.1
  37.1 15.2 %all_to_all.11.parts = f32[128,4,128]{2,1,0:T(4,128)S(1)} all-to-all(f32[128,4,128]{2,1,0:T(4,128)S(1)} %sum_parts.1), channel_id=1, replica_groups=mesh['dp'=8,'tensor'=16] {'dp','tensor'}, dimensions={0} | all-to-all | bytes 524288 | tf_op jit(solution)/shard_map/all_to_all | solution.py:279
  52.4 3.6 %finish.1 = (bf16[512,512]{1,0:T(8,128)(2,1)}, bf16[512,4096]{1,0:T(8,128)(2,1)}, f32[16,4096]{1,0:T(8,128)}) custom-call(f32[128,4,128]{2,1,0:T(4,128)S(1)} %all_to_all.11.parts, f32[16,512]{1,0:T(8,128)S(1)} %get-tuple-element.15.left_t, bf16[4096,16]{1,0:T(8,128)(2,1)S(1)} %turn_factor.1.after.factor_t, bf16[512,4096]{1,0:T(8,128)(2,1)S(1)} %get-tuple-element.12.merged), custom_call_target="tpu_custom_call" | custom-call | tf_op jit(solution)/shard_map/finish/pallas_call | solution.py:243
  (1 shorter events, 0.0 us)
Async XLA Ops:
  5.0 2.4 %collective-permute-start = (f32[16,512]{1,0:T(8,128)S(1)}, f32[16,512]{1,0:T(8,128)S(1)}, u32[]{:S(2)}, u32[]{:S(2)}) collective-permute-start(f32[16,512]{1,0:T(8,128)S(1)} %get-tuple-element.11), channel_id=1, source_target_pairs={{0,16},{16,0},{32,48},{48,32},{64,80},{80,64},{96,112},{112,96},{1... | collective-permute-start | bytes 98312 | tf_op jit(solution)/shard_map/ppermute | solution.py:272
  7.3 4.0 %collective-permute-start.3 = (f32[16,512]{1,0:T(8,128)S(1)}, f32[16,512]{1,0:T(8,128)S(1)}, u32[]{:S(2)}, u32[]{:S(2)}) collective-permute-start(f32[16,512]{1,0:T(8,128)S(1)} %add.3.own), channel_id=1, source_target_pairs={{0,96},{16,112},{32,64},{48,80},{64,32},{80,48},{96,0},{112,16},{1... | collective-permute-start | bytes 98312 | tf_op jit(solution)/shard_map/ppermute | solution.py:272
  9.9 4.3 %collective-permute-start.2 = (f32[16,512]{1,0:T(8,128)S(1)}, f32[16,512]{1,0:T(8,128)S(1)}, u32[]{:S(2)}, u32[]{:S(2)}) collective-permute-start(f32[16,512]{1,0:T(8,128)S(1)} %add.3.own), channel_id=1, source_target_pairs={{0,64},{16,80},{32,96},{48,112},{64,0},{80,16},{96,32},{112,48},{1... | collective-permute-start | bytes 98312 | tf_op jit(solution)/shard_map/ppermute | solution.py:272
  10.4 3.8 %collective-permute-start.1 = (f32[16,512]{1,0:T(8,128)S(1)}, f32[16,512]{1,0:T(8,128)S(1)}, u32[]{:S(2)}, u32[]{:S(2)}) collective-permute-start(f32[16,512]{1,0:T(8,128)S(1)} %add.3.own), channel_id=1, source_target_pairs={{0,32},{16,48},{32,0},{48,16},{64,96},{80,112},{96,64},{112,80},{1... | collective-permute-start | bytes 98312 | tf_op jit(solution)/shard_map/ppermute | solution.py:272

commit v7 on v6

--- a/solution.py
+++ b/solution.py
@@ -23,7 +23,7 @@
     return high, middle, (rest - middle.astype(F32)).astype(BF16)
 
 
-BLOCKS = ((0, 512), (512, 768), (1280, 1024), (2304, 1024), (3328, 512), (3840, 256))
+BLOCKS = ((0, 256), (256, 768), (1024, 768), (1792, 1024), (2816, 768), (3584, 384), (3968, 128))
 AHEAD = 3
 
 
@@ -51,9 +51,10 @@
     for i, (start, width) in enumerate(BLOCKS):
         for copy in copies(i):
             copy.wait()
-        if i + AHEAD < len(BLOCKS):
-            for copy in copies(i + AHEAD):
-                copy.start()
+        for later in (AHEAD, AHEAD + 1) if i == 0 else (i + AHEAD + 1,):
+            if later < len(BLOCKS):
+                for copy in copies(later):
+                    copy.start()
         if i == 0:
             q_copy.wait()
             factor[...] = q_v[...].astype(BF16)

time: 56.1 us -> 56 us (level)
  no operation moved by 1% of the time
where the time goes in v7:
time: 56 us; the launch traced here: 55.9 us
  blocking collectives  37.3 us (67%)
  Pallas kernels  9.11 us (16%)
  starting transfers between devices  4.75 us (8%)
  waiting for transfers between devices  4.09 us (7%)
  between operations  0.66 us (1%)
    all_to_all x2, blocking collectives, local(): parts = lax.all_to_all(parts, ('dp', 'tensor'), 0, 0, tiled=True)  37.3 us
    ppermute x4, starting transfers between devices, moved(): return lax.ppermute(value, 'dp', pairs)  4.75 us
    pallas_call x1, Pallas kernels, merge(): pl.pallas_call(merge_kernel, out_shape=(pltpu.VMEM((ROWS, COLS), BF16), p...  4.25 us
    ppermute x4, waiting for transfers between devices, moved(): return lax.ppermute(value, 'dp', pairs)  4.09 us
    pallas_call x1, Pallas kernels, finish(): pl.pallas_call(finish_kernel, out_shape=(jax.ShapeDtypeStruct((ROWS, OWN)...  3.58 us
  transfers between devices with their start and end apart: 4, of which 3 were waited for; matrix products, arithmetic and copies ran while one was open for 0% of the time, Pallas kernels for 1%

profile of v7, /device:TPU:1, one launch (start us, length us, event | category | flops | bytes accessed | tf_op | source)
XLA Modules:
  0.0 55.9 jit_solution(1749515007228730487)
XLA Ops:
  0.6 4.3 %merge_left.1 = (bf16[512,4096]{1,0:T(8,128)(2,1)S(1)}, f32[16,512]{1,0:T(8,128)S(1)}, bf16[16,4096]{1,0:T(8,128)(2,1)S(1)}) custom-call(bf16[512,4096]{1,0:T(8,128)(2,1)} %bitcast.3, bf16[512,4096]{1,0:T(8,128)(2,1)} %bitcast.4, f32[16,4096]{1,0:T(8,128)} %q.1), custom_call_target="tpu_custom_call" | custom-call | tf_op jit(solution)/shard_map/merge_left/pallas_call | solution.py:77
  4.9 1.5 %collective-permute-start = (f32[16,512]{1,0:T(8,128)S(1)}, f32[16,512]{1,0:T(8,128)S(1)}, u32[]{:S(2)}, u32[]{:S(2)}) collective-permute-start(f32[16,512]{1,0:T(8,128)S(1)} %get-tuple-element.11), channel_id=1, source_target_pairs={{0,16},{16,0},{32,48},{48,32},{64,80},{80,64},{96,112},{112,96},{1... | collective-permute-start | bytes 98312 | tf_op jit(solution)/shard_map/ppermute | solution.py:273
  6.4 0.9 %collective-permute-done = f32[16,512]{1,0:T(8,128)S(1)} collective-permute-done((f32[16,512]{1,0:T(8,128)S(1)}, f32[16,512]{1,0:T(8,128)S(1)}, u32[]{:S(2)}, u32[]{:S(2)}) %collective-permute-start) | collective-permute-done | bytes 32800 | tf_op jit(solution)/shard_map/ppermute | solution.py:273
  7.3 2.6 %collective-permute-start.3 = (f32[16,512]{1,0:T(8,128)S(1)}, f32[16,512]{1,0:T(8,128)S(1)}, u32[]{:S(2)}, u32[]{:S(2)}) collective-permute-start(f32[16,512]{1,0:T(8,128)S(1)} %add.3.own), channel_id=1, source_target_pairs={{0,96},{16,112},{32,64},{48,80},{64,32},{80,48},{96,0},{112,16},{1... | collective-permute-start | bytes 98312 | tf_op jit(solution)/shard_map/ppermute | solution.py:273
  9.8 0.5 collective-permute-start.2
  10.3 0.2 collective-permute-start.1
  10.5 0.3 turn_factor.1.after.factor_t
  10.9 0.4 collective-permute-done.3.three
  11.2 2.9 %collective-permute-done.2.two = f32[16,512]{1,0:T(8,128)S(1)} collective-permute-done((f32[16,512]{1,0:T(8,128)S(1)}, f32[16,512]{1,0:T(8,128)S(1)}, u32[]{:S(2)}, u32[]{:S(2)}) %collective-permute-start.2) | collective-permute-done | bytes 32800 | tf_op jit(solution)/shard_map/ppermute | solution.py:273
  14.1 0.0 collective-permute-done.1.one
  14.1 0.8 %right_parts.1 = (f32[16,512]{1,0:T(8,128)S(1)}, f32[128,4,128]{2,1,0:T(4,128)S(1)}) custom-call(f32[16,512]{1,0:T(8,128)S(1)} %add.3.own, f32[16,512]{1,0:T(8,128)S(1)} %collective-permute-done.1.one, f32[16,512]{1,0:T(8,128)S(1)} %collective-permute-done.2.two, f32[16,512]{1,0:T(8,128)S(1)} %collective-permute-done.3.three, ...), custom_call_target="tpu_custom_call" | custom-call | tf_op jit(solution)/shard_map/right_parts/pallas_call | solution.py:131
  14.9 22.0 %all_to_all.10.parts = f32[128,4,128]{2,1,0:T(4,128)S(1)} all-to-all(f32[128,4,128]{2,1,0:T(4,128)S(1)} %get-tuple-element.14), channel_id=1, replica_groups=mesh['dp'=8,'tensor'=16] {'dp','tensor'}, dimensions={0} | all-to-all | bytes 524288 | tf_op jit(solution)/shard_map/all_to_all | solution.py:278
  36.9 0.2 sum_parts.1
  37.1 15.2 %all_to_all.11.parts = f32[128,4,128]{2,1,0:T(4,128)S(1)} all-to-all(f32[128,4,128]{2,1,0:T(4,128)S(1)} %sum_parts.1), channel_id=1, replica_groups=mesh['dp'=8,'tensor'=16] {'dp','tensor'}, dimensions={0} | all-to-all | bytes 524288 | tf_op jit(solution)/shard_map/all_to_all | solution.py:280
  52.3 3.6 %finish.1 = (bf16[512,512]{1,0:T(8,128)(2,1)}, bf16[512,4096]{1,0:T(8,128)(2,1)}, f32[16,4096]{1,0:T(8,128)}) custom-call(f32[128,4,128]{2,1,0:T(4,128)S(1)} %all_to_all.11.parts, f32[16,512]{1,0:T(8,128)S(1)} %get-tuple-element.15.left_t, bf16[4096,16]{1,0:T(8,128)(2,1)S(1)} %turn_factor.1.after.factor_t, bf16[512,4096]{1,0:T(8,128)(2,1)S(1)} %get-tuple-element.12.merged), custom_call_target="tpu_custom_call" | custom-call | tf_op jit(solution)/shard_map/finish/pallas_call | solution.py:244
  (1 shorter events, 0.0 us)
Async XLA Ops:
  4.9 2.4 %collective-permute-start = (f32[16,512]{1,0:T(8,128)S(1)}, f32[16,512]{1,0:T(8,128)S(1)}, u32[]{:S(2)}, u32[]{:S(2)}) collective-permute-start(f32[16,512]{1,0:T(8,128)S(1)} %get-tuple-element.11), channel_id=1, source_target_pairs={{0,16},{16,0},{32,48},{48,32},{64,80},{80,64},{96,112},{112,96},{1... | collective-permute-start | bytes 98312 | tf_op jit(solution)/shard_map/ppermute | solution.py:273
  7.3 4.0 %collective-permute-start.3 = (f32[16,512]{1,0:T(8,128)S(1)}, f32[16,512]{1,0:T(8,128)S(1)}, u32[]{:S(2)}, u32[]{:S(2)}) collective-permute-start(f32[16,512]{1,0:T(8,128)S(1)} %add.3.own), channel_id=1, source_target_pairs={{0,96},{16,112},{32,64},{48,80},{64,32},{80,48},{96,0},{112,16},{1... | collective-permute-start | bytes 98312 | tf_op jit(solution)/shard_map/ppermute | solution.py:273
  9.8 4.3 %collective-permute-start.2 = (f32[16,512]{1,0:T(8,128)S(1)}, f32[16,512]{1,0:T(8,128)S(1)}, u32[]{:S(2)}, u32[]{:S(2)}) collective-permute-start(f32[16,512]{1,0:T(8,128)S(1)} %add.3.own), channel_id=1, source_target_pairs={{0,64},{16,80},{32,96},{48,112},{64,0},{80,16},{96,32},{112,48},{1... | collective-permute-start | bytes 98312 | tf_op jit(solution)/shard_map/ppermute | solution.py:273
  10.3 3.8 %collective-permute-start.1 = (f32[16,512]{1,0:T(8,128)S(1)}, f32[16,512]{1,0:T(8,128)S(1)}, u32[]{:S(2)}, u32[]{:S(2)}) collective-permute-start(f32[16,512]{1,0:T(8,128)S(1)} %add.3.own), channel_id=1, source_target_pairs={{0,32},{16,48},{32,0},{48,16},{64,96},{80,112},{96,64},{112,80},{1... | collective-permute-start | bytes 98312 | tf_op jit(solution)/shard_map/ppermute | solution.py:273
